TPU v7x, 32 devices: a whole 2x2x4 slice. The times are simulated.
32 devices in a mesh: cells: 4 (over y, x), region: 8 (over z, core).
Axes of the slice: x: 2, y: 2, z: 4, core: 2. Of those that a mesh axis runs over, the one named last changes fastest.
Arguments:
- cell_shape: bfloat16 [32, 3, 544], P(('cells', 'region')), may hold values from -6 to 6
- upsample: bfloat16 [544, 2112], replicated, may hold values from -0.25 to 0.25
- bending: bfloat16 [544, 2112], replicated, may hold values from -0.25 to 0.25
- to_density: bfloat16 [2112, 152], replicated, may hold values from -0.125 to 0.125
- translate: bfloat16 [456, 456], replicated, may hold values from -0.25 to 0.25
- evaluate: bfloat16 [152, 2112], replicated, may hold values from -0.5 to 0.5
- smoothing: bfloat16 [2112, 544], replicated, may hold values from -0.125 to 0.125
- block_owner: int32 [8448, 1], P(('cells', 'region')), may hold values from 0 to 3; in each aligned block of 264 rows (0 to 263, 264 to 527, ...) at most 68 rows name the same one
- block_octant: int32 [8448], P(('cells', 'region')), may hold values from 0 to 7
- far_list: int32 [32, 8], P(('cells', 'region')), may hold values from 0 to 63
Outputs:
- velocity: float32 [32, 3, 544], P(('cells', 'region'))
Inputs may be any that keep to these rules, and one draw needn't show every extreme that they name: `block_owner`: among the 264 blocks of one device no owner is named more than 68 times, and in some device's blocks one owner is named exactly 68 times.
All inputs are finite; a program needn't handle non-finite values.
Results may differ from a plain program's by a relative error of at most 0.0063.
Values may be sent and summed in bfloat16 or wider, within the bound.
No kernel may reach another device: no remote copies, remote signals or barrier semaphores. Data moves between devices by JAX's collectives and lax.ppermute only.
A program may use at most 64 MiB of HBM per device.

v0:
```python
from functools import partial

import jax
import jax.numpy as jnp
from jax import lax
from jax.sharding import PartitionSpec as P

P_COARSE = 544
P_FINE = 2112
EQ_PTS = 152
EQUIV = 456
BLK = 8
OCT_DEV = 2


EPSILON_SQ = 0.0625
STOKES_SCALE = 1.0 / (8.0 * 3.141592653589793)


def stokeslet(targets, sources, strength):
    diff_x = targets[0][:, None] - sources[0][None, :]
    diff_y = targets[1][:, None] - sources[1][None, :]
    diff_z = targets[2][:, None] - sources[2][None, :]
    radius_sq = diff_x * diff_x + diff_y * diff_y + diff_z * diff_z + EPSILON_SQ
    inverse = lax.rsqrt(radius_sq)
    cubed = inverse * inverse * inverse
    direct = (radius_sq + EPSILON_SQ) * cubed
    radial = (
        diff_x * strength[0][None, :]
        + diff_y * strength[1][None, :]
        + diff_z * strength[2][None, :]
    ) * cubed
    vel_x = jnp.sum(direct * strength[0][None, :] + diff_x * radial, axis=1)
    vel_y = jnp.sum(direct * strength[1][None, :] + diff_y * radial, axis=1)
    vel_z = jnp.sum(direct * strength[2][None, :] + diff_z * radial, axis=1)
    return jnp.stack([vel_x, vel_y, vel_z]) * STOKES_SCALE


def near_field(leaf_points):
    sources = leaf_points[:3].astype(jnp.float32)
    strength = leaf_points[3:].astype(jnp.float32)
    point_total = sources.shape[1]
    padding = -point_total % 256
    padded = jnp.pad(sources, ((0, 0), (0, padding)))
    tile_set = padded.reshape(3, -1, 256).transpose(1, 0, 2)
    result = lax.map(partial(stokeslet, sources=sources, strength=strength), tile_set)
    return result.transpose(1, 0, 2).reshape(3, -1)[:, :point_total]


def slot_numbers(owner, owners_count, capacity):
    onehot = (owner[:, None] == jnp.arange(owners_count, dtype=jnp.int32)[None, :]).astype(
        jnp.int32
    )
    before = jnp.cumsum(onehot, axis=0) - onehot
    slot_rank = jnp.sum(before * onehot, axis=1)
    return owner * capacity + slot_rank


def same_rows(row_ids):
    return row_ids


def add_listed(portion, listed, id_map):
    row_ids = jnp.arange(portion.shape[0], dtype=jnp.int32)
    octant_id = id_map(row_ids)
    counts = jnp.sum((listed[:, :, None] == octant_id[None, None, :]).astype(jnp.float32), axis=1)
    return jnp.dot(counts.astype(jnp.bfloat16), portion, preferred_element_type=jnp.float32)


def on_device(
    cell_shape,
    upsample,
    bending,
    to_density,
    translate,
    evaluate,
    smoothing,
    block_owner,
    block_octant,
    far_list,
):
    cell_count = cell_shape.shape[0]
    owners_count = lax.axis_size("cells")
    per_cell = P_FINE // BLK
    block_count = block_owner.shape[0]
    capacity = block_count // owners_count + 2
    coarse = cell_shape.reshape(cell_count * 3, P_COARSE)
    points = (
        jnp.dot(coarse, upsample, preferred_element_type=jnp.float32)
        .astype(jnp.bfloat16)
        .reshape(cell_count, 3, P_FINE)
    )
    forces = (
        jnp.dot(coarse, bending, preferred_element_type=jnp.float32)
        .astype(jnp.bfloat16)
        .reshape(cell_count, 3, P_FINE)
    )
    stacked = jnp.concatenate([points, forces], axis=1)
    blocks = (
        stacked.reshape(cell_count, 6, per_cell, BLK)
        .transpose(0, 2, 1, 3)
        .reshape(block_count, 6, BLK)
    )
    slot_index = slot_numbers(block_owner[:, 0], owners_count, capacity)
    outgoing = jnp.zeros((owners_count * capacity, 6, BLK), jnp.bfloat16).at[slot_index].set(blocks)
    outgoing = (
        outgoing.reshape(owners_count, capacity, 6, BLK)
        .transpose(0, 2, 1, 3)
        .reshape(owners_count, 6, capacity * BLK)
    )
    incoming = lax.all_to_all(outgoing, "cells", split_axis=0, concat_axis=0, tiled=True)
    leaf_points = incoming.transpose(1, 0, 2).reshape(6, owners_count * capacity * BLK)
    near_vel = near_field(leaf_points)
    replies = near_vel.reshape(3, owners_count, capacity * BLK).transpose(1, 0, 2)
    returned = lax.all_to_all(replies, "cells", split_axis=0, concat_axis=0, tiled=True)
    returned = (
        returned.reshape(owners_count, 3, capacity, BLK)
        .transpose(0, 2, 1, 3)
        .reshape(owners_count * capacity, 3, BLK)
    )
    own_blocks = returned[slot_index]
    near_points = (
        own_blocks.reshape(cell_count, per_cell, 3, BLK)
        .transpose(0, 2, 1, 3)
        .reshape(cell_count, 3, P_FINE)
    )
    octant_local = OCT_DEV * owners_count
    octant_blocks = block_octant.reshape(cell_count, per_cell, 1)
    point_octant = jnp.broadcast_to(octant_blocks, (cell_count, per_cell, BLK)).reshape(
        cell_count, P_FINE
    )
    choose = point_octant[None] == jnp.arange(octant_local, dtype=jnp.int32)[:, None, None]
    masked = jnp.where(choose[:, :, None, :], forces[None], jnp.zeros((), jnp.bfloat16))
    product = jnp.dot(masked.reshape(-1, P_FINE), to_density, preferred_element_type=jnp.float32)
    density_part = jnp.sum(product.reshape(octant_local, cell_count, EQUIV), axis=1)
    summed = lax.psum(density_part, "cells")
    expansion = jnp.dot(
        summed.astype(jnp.bfloat16), translate, preferred_element_type=jnp.float32
    ).astype(jnp.bfloat16)
    far_sum = add_listed(
        lax.all_gather(expansion, "region", axis=0, tiled=True), listed=far_list, id_map=same_rows
    )
    far_round = far_sum.astype(jnp.bfloat16).reshape(cell_count * 3, EQ_PTS)
    far_velocity = jnp.dot(far_round, evaluate, preferred_element_type=jnp.float32).reshape(
        cell_count, 3, P_FINE
    )
    total = (near_points + far_velocity).astype(jnp.bfloat16)
    velocity = jnp.dot(
        total.reshape(cell_count * 3, P_FINE), smoothing, preferred_element_type=jnp.float32
    )
    return velocity.reshape(cell_count, 3, P_COARSE)


def solution(mesh):
    return jax.shard_map(
        on_device,
        mesh=mesh,
        in_specs=(
            P(("cells", "region"), None, None),
            P(),
            P(),
            P(),
            P(),
            P(),
            P(),
            P(("cells", "region"), None),
            P(("cells", "region")),
            P(("cells", "region"), None),
        ),
        out_specs=P(("cells", "region"), None, None),
        check_vma=False,
    )
```

profile of v0, /device:TPU:0, one launch (start us, length us, event | category | flops | bytes accessed | tf_op | source)
XLA Modules:
  0.0 99.9 jit_solution(6390410222752302229)
XLA Ops:
  0.0 0.8 reduce.7
  0.9 1.2 %reduce-window.6 = s32[4,3,128]{2,1,0:T(4,128)S(1)} reduce-window(s32[4,3,128]{2,1,0:T(4,128)S(1)} %copy.67, s32[]{:T(128)} %constant.50.clone.1), window={size=1x1x128 pad=0_0x0_0x127_0}, to_apply=%region_0.0 | reduce-window | flops 195072 | bytes 12292 | tf_op jit(solution)/shard_map/reduce-window
  2.1 0.2 slice_reduce_fusion.6
  2.3 0.2 reduce-window.9
  2.6 0.7 fusion.24
  3.3 1.1 %convolution_convert_fusion = bf16[3,2112]{1,0:T(4,128)(2,1)S(1)} fusion(bf16[544,2112]{1,0:T(8,128)(2,1)S(1)} %copy-done, bf16[1,3,544]{2,1,0:T(4,128)(2,1)} %param.12), kind=kOutput, calls=%fused_computation.40 | convolution fusion | flops 6899904 | bytes 2313792 | tf_op jit(solution)/shard_map/dot_general | solution.py:94
  4.4 0.2 concatenate.19
  4.7 0.1 copy.69
  4.8 2.1 %convolution_convert_fusion.1 = bf16[3,2112]{1,0:T(4,128)(2,1)S(1)} fusion(bf16[544,2112]{1,0:T(8,128)(2,1)} %param.13, bf16[1,3,544]{2,1,0:T(4,128)(2,1)S(1)} %copy-done.2), kind=kOutput, calls=%fused_computation.41 | convolution fusion | flops 6899904 | bytes 2313792 | tf_op jit(solution)/shard_map/dot_general | solution.py:89
  6.9 0.2 concatenate.18
  7.2 0.1 copy.68
  7.4 0.3 copy.70
  7.8 8.6 %scatter_fusion = bf16[272,6,8]{2,1,0:T(8,128)(2,1)S(1)} fusion(bf16[272,6,8]{2,1,0:T(8,128)(2,1)S(1)} %broadcast_in_dim.41, s32[264]{0:T(512)S(1)} %fusion.24, bf16[264,6,8]{2,1,0:T(8,128)(2,1)S(1)} %copy.70), kind=kCustom, calls=%fused_computation.1 | custom fusion | bytes 77088 | tf_op jit(solution)/shard_map/scatter | solution.py:105
  16.5 0.4 copy.82
  16.8 0.3 copy.83
  17.1 1.0 reshape.261
  18.1 5.2 %all-to-all-start = ((bf16[4,6,544]{2,1,0:T(8,128)(2,1)}), bf16[4,6,544]{2,1,0:T(8,128)(2,1)S(1)}, u32[]{:S(2)}, u32[]{:S(2)}) async-start(bf16[4,6,544]{2,1,0:T(8,128)(2,1)} %reshape.261), calls=%async_computation | async-start | bytes 81920 | tf_op jit(solution)/shard_map/all_to_all | solution.py:111
  23.7 1.4 %fusion.28 = f32[24,152]{1,0:T(8,128)S(1)} fusion(bf16[24,2112]{1,0:T(8,128)(2,1)S(1)} %select_n.17, bf16[2112,152]{0,1:T(8,128)(2,1)} %param.15), kind=kOutput, calls=%fused_computation.71 | convolution fusion | flops 15409152 | bytes 758016 | tf_op jit(solution)/shard_map/dot_general | solution.py:134
  25.2 16.5 %psum.7 = bf16[8,456]{1,0:T(8,128)(2,1)S(1)} all-reduce(f32[8,456]{1,0:T(8,128)S(1)} %reduce_sum.65), channel_id=1, replica_groups=mesh['cells'=4,'region'=8] {'cells'}, use_global_device_ids=true, to_apply=%region_10.11 | all-reduce | flops 3648 | bytes 21888 | tf_op jit(solution)/shard_map/psum | solution.py:136
  41.7 0.2 convolution_convert_fusion.2
  41.9 14.2 %all_gather.3 = bf16[64,456]{1,0:T(8,128)(2,1)S(1)} all-gather(bf16[8,456]{1,0:T(8,128)(2,1)S(1)} %convolution_convert_fusion.2), channel_id=1, replica_groups=mesh['cells'=4,'region'=8] {'region'}, dimensions={0}, use_global_device_ids=true | all-gather | bytes 65664 | tf_op jit(solution)/shard_map/all_gather | solution.py:141
  56.6 28.4 %while.12 = (s32[]{:T(128)}, f32[9,3,256]{2,1,0:T(4,128)S(1)}, f32[9,3,256]{2,0,1:T(8,128)S(1)}, f32[3,2176]{1,0:T(4,128)S(1)}, f32[3,2176]{1,0:T(4,128)S(1)}, /*index=5*/s32[]{:T(128)}, s32[]{:T(128)}, s32[]{}, s32[]{}) while((s32[]{:T(128)}, f32[9,3,256]{2,1,0:T(4,128)S(1)}, f32[9,3,256]{2,0,1:T(8,128)S(1)}, f32[3,2176]{1,0:T(4,128)S(1)}, ...), condition=%wide.region_8.9_spmd, body=%wide.region_4.0_spmd.sunk | while | flops 17270276 | bytes 176261 | solution.py:46
  56.6 0.1 slice_reduce_fusion.8
  56.8 3.0 %fusion.41 = (f32[256]{0:T(256)S(1)}, f32[256]{0:T(256)S(1)}, f32[256]{0:T(256)S(1)}) fusion(f32[2176]{0:T(1024)S(1)} %get-tuple-element.166, f32[2176]{0:T(1024)S(1)} %get-tuple-element.167, f32[256]{0:T(256)S(1)} %bitcast.92, f32[2176]{0:T(1024)S(1)} %get-tuple-element.169, f32[256]{0:T(256)S(1)} %bitcast.93, f32[2176]{0:T(1024)S(1)} %get-tuple-element.171, ...), kind=kLoop, calls=%fused_computation.18.clone.1 | loop fusion | flops 17267968 | bytes 58368 | tf_op jit(solution)/shard_map/while/body/eval_jaxpr/reduce_sum | solution.py:33
  59.8 0.1 slice_reduce_fusion.8
  59.9 3.0 %fusion.41 = (f32[256]{0:T(256)S(1)}, f32[256]{0:T(256)S(1)}, f32[256]{0:T(256)S(1)}) fusion(f32[2176]{0:T(1024)S(1)} %get-tuple-element.166, f32[2176]{0:T(1024)S(1)} %get-tuple-element.167, f32[256]{0:T(256)S(1)} %bitcast.92, f32[2176]{0:T(1024)S(1)} %get-tuple-element.169, f32[256]{0:T(256)S(1)} %bitcast.93, f32[2176]{0:T(1024)S(1)} %get-tuple-element.171, ...), kind=kLoop, calls=%fused_computation.18.clone.1 | loop fusion | flops 17267968 | bytes 58368 | tf_op jit(solution)/shard_map/while/body/eval_jaxpr/reduce_sum | solution.py:33
  62.9 0.1 slice_reduce_fusion.8
  63.1 3.0 %fusion.41 = (f32[256]{0:T(256)S(1)}, f32[256]{0:T(256)S(1)}, f32[256]{0:T(256)S(1)}) fusion(f32[2176]{0:T(1024)S(1)} %get-tuple-element.166, f32[2176]{0:T(1024)S(1)} %get-tuple-element.167, f32[256]{0:T(256)S(1)} %bitcast.92, f32[2176]{0:T(1024)S(1)} %get-tuple-element.169, f32[256]{0:T(256)S(1)} %bitcast.93, f32[2176]{0:T(1024)S(1)} %get-tuple-element.171, ...), kind=kLoop, calls=%fused_computation.18.clone.1 | loop fusion | flops 17267968 | bytes 58368 | tf_op jit(solution)/shard_map/while/body/eval_jaxpr/reduce_sum | solution.py:33
  66.1 0.1 slice_reduce_fusion.8
  66.2 3.0 %fusion.41 = (f32[256]{0:T(256)S(1)}, f32[256]{0:T(256)S(1)}, f32[256]{0:T(256)S(1)}) fusion(f32[2176]{0:T(1024)S(1)} %get-tuple-element.166, f32[2176]{0:T(1024)S(1)} %get-tuple-element.167, f32[256]{0:T(256)S(1)} %bitcast.92, f32[2176]{0:T(1024)S(1)} %get-tuple-element.169, f32[256]{0:T(256)S(1)} %bitcast.93, f32[2176]{0:T(1024)S(1)} %get-tuple-element.171, ...), kind=kLoop, calls=%fused_computation.18.clone.1 | loop fusion | flops 17267968 | bytes 58368 | tf_op jit(solution)/shard_map/while/body/eval_jaxpr/reduce_sum | solution.py:33
  69.2 0.1 slice_reduce_fusion.8
  69.4 3.0 %fusion.41 = (f32[256]{0:T(256)S(1)}, f32[256]{0:T(256)S(1)}, f32[256]{0:T(256)S(1)}) fusion(f32[2176]{0:T(1024)S(1)} %get-tuple-element.166, f32[2176]{0:T(1024)S(1)} %get-tuple-element.167, f32[256]{0:T(256)S(1)} %bitcast.92, f32[2176]{0:T(1024)S(1)} %get-tuple-element.169, f32[256]{0:T(256)S(1)} %bitcast.93, f32[2176]{0:T(1024)S(1)} %get-tuple-element.171, ...), kind=kLoop, calls=%fused_computation.18.clone.1 | loop fusion | flops 17267968 | bytes 58368 | tf_op jit(solution)/shard_map/while/body/eval_jaxpr/reduce_sum | solution.py:33
  72.4 0.1 slice_reduce_fusion.8
  72.6 3.0 %fusion.41 = (f32[256]{0:T(256)S(1)}, f32[256]{0:T(256)S(1)}, f32[256]{0:T(256)S(1)}) fusion(f32[2176]{0:T(1024)S(1)} %get-tuple-element.166, f32[2176]{0:T(1024)S(1)} %get-tuple-element.167, f32[256]{0:T(256)S(1)} %bitcast.92, f32[2176]{0:T(1024)S(1)} %get-tuple-element.169, f32[256]{0:T(256)S(1)} %bitcast.93, f32[2176]{0:T(1024)S(1)} %get-tuple-element.171, ...), kind=kLoop, calls=%fused_computation.18.clone.1 | loop fusion | flops 17267968 | bytes 58368 | tf_op jit(solution)/shard_map/while/body/eval_jaxpr/reduce_sum | solution.py:33
  75.5 0.1 slice_reduce_fusion.8
  75.7 3.0 %fusion.41 = (f32[256]{0:T(256)S(1)}, f32[256]{0:T(256)S(1)}, f32[256]{0:T(256)S(1)}) fusion(f32[2176]{0:T(1024)S(1)} %get-tuple-element.166, f32[2176]{0:T(1024)S(1)} %get-tuple-element.167, f32[256]{0:T(256)S(1)} %bitcast.92, f32[2176]{0:T(1024)S(1)} %get-tuple-element.169, f32[256]{0:T(256)S(1)} %bitcast.93, f32[2176]{0:T(1024)S(1)} %get-tuple-element.171, ...), kind=kLoop, calls=%fused_computation.18.clone.1 | loop fusion | flops 17267968 | bytes 58368 | tf_op jit(solution)/shard_map/while/body/eval_jaxpr/reduce_sum | solution.py:33
  78.7 0.1 slice_reduce_fusion.8
  78.9 3.0 %fusion.41 = (f32[256]{0:T(256)S(1)}, f32[256]{0:T(256)S(1)}, f32[256]{0:T(256)S(1)}) fusion(f32[2176]{0:T(1024)S(1)} %get-tuple-element.166, f32[2176]{0:T(1024)S(1)} %get-tuple-element.167, f32[256]{0:T(256)S(1)} %bitcast.92, f32[2176]{0:T(1024)S(1)} %get-tuple-element.169, f32[256]{0:T(256)S(1)} %bitcast.93, f32[2176]{0:T(1024)S(1)} %get-tuple-element.171, ...), kind=kLoop, calls=%fused_computation.18.clone.1 | loop fusion | flops 17267968 | bytes 58368 | tf_op jit(solution)/shard_map/while/body/eval_jaxpr/reduce_sum | solution.py:33
  82.0 3.0 %fusion.41 = (f32[256]{0:T(256)S(1)}, f32[256]{0:T(256)S(1)}, f32[256]{0:T(256)S(1)}) fusion(f32[2176]{0:T(1024)S(1)} %get-tuple-element.166, f32[2176]{0:T(1024)S(1)} %get-tuple-element.167, f32[256]{0:T(256)S(1)} %bitcast.92, f32[2176]{0:T(1024)S(1)} %get-tuple-element.169, f32[256]{0:T(256)S(1)} %bitcast.93, f32[2176]{0:T(1024)S(1)} %get-tuple-element.171, ...), kind=kLoop, calls=%fused_computation.18.clone.1 | loop fusion | flops 17267968 | bytes 58368 | tf_op jit(solution)/shard_map/while/body/eval_jaxpr/reduce_sum | solution.py:33
  85.1 0.6 copy.76
  85.7 3.3 %all-to-all-start.1 = ((f32[4,3,544]{2,1,0:T(4,128)}), f32[4,3,544]{2,1,0:T(4,128)S(1)}, u32[]{:S(2)}, u32[]{:S(2)}) async-start(f32[4,3,544]{2,1,0:T(4,128)} %copy.76), calls=%async_computation.1 | async-start | bytes 81920 | tf_op jit(solution)/shard_map/all_to_all | solution.py:115
  89.1 4.6 %all-to-all-done.1 = f32[4,3,544]{2,1,0:T(4,128)S(1)} async-done(((f32[4,3,544]{2,1,0:T(4,128)}), f32[4,3,544]{2,1,0:T(4,128)S(1)}, u32[]{:S(2)}, u32[]{:S(2)}) %all-to-all-start.1) | async-done | bytes 26144 | tf_op jit(solution)/shard_map/all_to_all | solution.py:115
  93.8 0.2 reshape.234
  94.0 0.3 copy.84
  94.3 2.0 %gather_fusion = f32[264,3,8]{2,1,0:T(4,128)S(1)} fusion(f32[272,3,8]{2,1,0:T(4,128)S(1)} %bitcast.83, s32[1024]{0:T(1024)S(1)} %pad_clamp_fusion), kind=kCustom, calls=%fused_computation | custom fusion | bytes 51744 | tf_op jit(solution)/shard_map/gather | solution.py:121
  96.3 0.2 reshape.237
  96.5 2.8 %fusion.18 = f32[1,3,544]{2,1,0:T(4,128)S(1)} fusion(bf16[2112,544]{0,1:T(8,128)(2,1)} %param.18, f32[3,2112]{1,0:T(4,128)S(1)} %reshape.237, bf16[3,152]{1,0:T(4,128)(2,1)S(1)} %reshape.238, bf16[152,2112]{1,0:T(8,128)(2,1)} %param.17), kind=kOutput, calls=%fused_computation.44 | convolution fusion | flops 8832384 | bytes 2972688 | tf_op jit(solution)/shard_map/dot_general | solution.py:148
  99.3 0.6 copy.81
  (60 shorter events, 2.0 us)
Async XLA Ops:
  0.0 3.3 %copy-start = (bf16[544,2112]{1,0:T(8,128)(2,1)S(1)}, bf16[544,2112]{1,0:T(8,128)(2,1)}, u32[]{:S(2)}) copy-start(bf16[544,2112]{1,0:T(8,128)(2,1)} %param.14) | copy-start | bytes 6893572
  0.0 4.8 %copy-start.2 = (bf16[1,3,544]{2,1,0:T(4,128)(2,1)S(1)}, bf16[1,3,544]{2,1,0:T(4,128)(2,1)}, u32[]{:S(2)}) copy-start(bf16[1,3,544]{2,1,0:T(4,128)(2,1)} %param.12) | copy-start | bytes 9796
  7.4 15.9 %copy-start.3 = (s32[264]{0:T(512)S(1)}, s32[264]{0:T(512)}, u32[]{:S(2)}) copy-start(s32[264]{0:T(512)} %param.20) | copy-start | bytes 3172
  16.4 25.3 %copy-start.1 = (bf16[456,456]{1,0:T(8,128)(2,1)S(1)}, bf16[456,456]{1,0:T(8,128)(2,1)}, u32[]{:S(2)}) copy-start(bf16[456,456]{1,0:T(8,128)(2,1)} %param.16) | copy-start | bytes 1247620
  16.5 39.6 %copy-start.4 = (s32[1,8]{1,0:T(1,128)S(1)}, s32[1,8]{1,0:T(1,128)}, u32[]{:S(2)}) copy-start(s32[1,8]{1,0:T(1,128)} %param.21) | copy-start | bytes 100
  18.1 38.2 %all-to-all-start = ((bf16[4,6,544]{2,1,0:T(8,128)(2,1)}), bf16[4,6,544]{2,1,0:T(8,128)(2,1)S(1)}, u32[]{:S(2)}, u32[]{:S(2)}) async-start(bf16[4,6,544]{2,1,0:T(8,128)(2,1)} %reshape.261), calls=%async_computation | async-start | bytes 81920 | tf_op jit(solution)/shard_map/all_to_all | solution.py:111
  85.7 8.0 %all-to-all-start.1 = ((f32[4,3,544]{2,1,0:T(4,128)}), f32[4,3,544]{2,1,0:T(4,128)S(1)}, u32[]{:S(2)}, u32[]{:S(2)}) async-start(f32[4,3,544]{2,1,0:T(4,128)} %copy.76), calls=%async_computation.1 | async-start | bytes 81920 | tf_op jit(solution)/shard_map/all_to_all | solution.py:115
where the time goes:
time: 100 us; the launch traced here: 99.9 us
  blocking collectives  30.7 us (31%)
  other arithmetic  30.1 us (30%)
  local copies, waits for them, and re-layouts  17.9 us (18%)
  starting transfers between devices  8.43 us (8%)
  matrix products  7.63 us (8%)
  waiting for transfers between devices  4.64 us (5%)
    reduce_sum x9, other arithmetic, stokeslet(): vel_x = jnp.sum(direct * strength[0][None, :] + diff_x * radial, axis=1)  26.6 us
    psum x1, blocking collectives, on_device(): summed = lax.psum(density_part, 'cells')  16.5 us
    all_gather x1, blocking collectives, on_device(): lax.all_gather(expansion, 'region', axis=0, tiled=True)  14.2 us
    scatter x1, local copies, waits for them, and re-layouts, on_device(): jnp.zeros((owners_count * capacity, 6, BLK), jnp.bfloat16).at[slot_index]  8.62 us
    all_to_all x1, starting transfers between devices, on_device(): lax.all_to_all(outgoing, 'cells', split_axis=0, concat_axis=0, tiled=True)  5.16 us
    all_to_all x1, waiting for transfers between devices, on_device(): lax.all_to_all(replies, 'cells', split_axis=0, concat_axis=0, tiled=True)  4.63 us
    all_to_all x1, starting transfers between devices, on_device(): lax.all_to_all(replies, 'cells', split_axis=0, concat_axis=0, tiled=True)  3.27 us
    dot_general x1, matrix products, on_device(): jnp.dot(total.reshape(cell_count * 3, P_FINE), smoothing, preferred_eleme...  2.76 us
  transfers between devices with their start and end apart: 2, of which 1 were waited for; matrix products, arithmetic and copies ran while one was open for 2% of the time, Pallas kernels for 0%

commit v1 on v0

v1 whole, which is shorter than its diff:
```python
import functools

import jax
import jax.numpy as jnp
from jax import lax
from jax.experimental import pallas as pl
from jax.experimental.pallas import tpu as pltpu
from jax.sharding import PartitionSpec as P

EPSILON_SQ = 0.0625
STOKES_SCALE = 1.0 / (8.0 * 3.141592653589793)
EXPAND_LIMIT = 256.0
TILE = 256
OCTANTS_PER_OWNER = 2
F32 = jnp.float32
BF16 = jnp.bfloat16
LANES = (((1,), (1,)), ((), ()))


def iota(shape, dim):
    return lax.broadcasted_iota(jnp.int32, shape, dim)


def dot(a, b):
    return jnp.dot(a, b, preferred_element_type=F32)


def dot_lanes(a, b):
    return lax.dot_general(a, b, LANES, preferred_element_type=F32)


def split_bf16(x):
    high = x.astype(BF16)
    return high, (x - high.astype(F32)).astype(BF16)


def pack_kernel(cell_ref, owner_ref, octant_ref, pack_ref, spread_ref):
    nb = owner_ref.shape[1]
    width = cell_ref.shape[1]
    pack_ref[0:3, :] = cell_ref[...]
    row = jnp.concatenate(
        [
            owner_ref[...].astype(F32),
            octant_ref[...].astype(F32),
            jnp.zeros((1, width - 2 * nb), F32),
        ],
        axis=1,
    )
    pack_ref[3:4, :] = row.astype(BF16)
    spread_ref[...] = jnp.broadcast_to(pack_ref[...][None], spread_ref.shape)


def interleave_matrix(blk):
    group = TILE // blk
    point, lane = iota((TILE, TILE), 0), iota((TILE, TILE), 1)
    return ((point % blk == lane // group) & (point // blk == lane % group)).astype(BF16)


def source_columns(rows):
    forces = jnp.concatenate([rows[4:8], rows[4:8]], axis=0)
    places = jnp.concatenate([rows[0:4], rows[0:4]], axis=0)
    upper = iota(rows.shape, 0) < 4
    groups = []
    square = jnp.zeros_like(rows)
    inner = jnp.zeros_like(rows)
    for k in range(3):
        x_k = jnp.broadcast_to(rows[k : k + 1], rows.shape)
        product = x_k * forces
        high = product.astype(BF16).astype(F32)
        groups.append(jnp.where(upper, high, product - high))
        square = square + x_k * x_k
        inner = inner + x_k * rows[4 + k : 5 + k]
    rest = square * forces + inner * places
    high = rest.astype(BF16).astype(F32)
    middle = (rest - high).astype(BF16).astype(F32)
    groups.append(jnp.where(upper, high, middle))
    groups.append(jnp.where(upper, rest - high - middle, forces))
    return jnp.concatenate(groups, axis=0).astype(BF16)


def squared_distance(spread, rows, start, stop):
    total = None
    diffs = []
    for k in range(3):
        diff = jnp.concatenate([spread[k]] * ((stop - start) // 128), axis=1) - rows[k : k + 1, start:stop]
        diffs.append(diff)
        term = diff * diff
        total = term + EPSILON_SQ if total is None else total + term
    return total, diffs


def expanded_sums(spread, rows, targets):
    columns = source_columns(rows)
    sums = None
    for start in range(0, rows.shape[1], TILE):
        stop = min(start + TILE, rows.shape[1])
        dist, _ = squared_distance(spread, rows, start, stop)
        inverse = lax.rsqrt(dist)
        cubed = (inverse * inverse * inverse).astype(BF16)
        part = dot_lanes(columns[:, start:stop], cubed)
        sums = part if sums is None else sums + part
    place = targets[0:4]
    moment = [sums[8 * k : 8 * k + 4] + sums[8 * k + 4 : 8 * k + 8] for k in range(3)]
    rest = sums[24:28] + sums[28:32] + sums[32:36]
    force = sums[36:40]
    square = jnp.sum(place * place, axis=0, keepdims=True)
    along = jnp.sum(place * force, axis=0, keepdims=True)
    trace = moment[0][0:1] + moment[1][1:2] + moment[2][2:3]
    cross = [jnp.sum(place * moment[k], axis=0, keepdims=True) for k in range(3)]
    cross = jnp.concatenate(cross + [jnp.zeros_like(trace)], axis=0)
    weighted = place[0:1] * moment[0] + place[1:2] * moment[1] + place[2:3] * moment[2]
    return (
        (square + 2.0 * EPSILON_SQ) * force + rest - 2.0 * weighted + place * (along - trace) - cross
    )


def direct_sums(spread, rows, targets):
    strength = rows[4:8].astype(BF16)
    ones = jnp.ones((1, rows.shape[1]), F32)
    places = jnp.concatenate([rows[0:3], ones], axis=0).astype(BF16)
    sums = None
    for start in range(0, rows.shape[1], TILE):
        stop = min(start + TILE, rows.shape[1])
        dist, diffs = squared_distance(spread, rows, start, stop)
        inverse = lax.rsqrt(dist)
        cubed = inverse * inverse * inverse
        direct = ((dist + EPSILON_SQ) * cubed).astype(BF16)
        along = sum(diffs[k] * rows[4 + k : 5 + k, start:stop] for k in range(3))
        radial = (along * cubed).astype(BF16)
        near = dot_lanes(strength[:, start:stop], direct)
        away = dot_lanes(places[:, start:stop], radial)
        part = jnp.concatenate([near, away], axis=0)
        sums = part if sums is None else sums + part
    return sums[0:4] + targets[0:4] * sums[7:8] - sums[4:8]


def near_kernel(blk, *refs):
    *pack_refs, up_ref, bend_ref, out_ref = refs
    packs = []
    for ref in pack_refs:
        if len(ref.shape) == 2:
            packs.append(ref[...])
        else:
            packs += [ref[i] for i in range(ref.shape[0])]
    cells = len(packs)
    fine = up_ref.shape[1]
    nb = fine // blk
    capacity = nb // cells + 2
    spots = cells * capacity
    group = TILE // blk
    tiles = -(-fine // TILE)
    point_rows, force_rows, owners = [], [], []
    for pack in packs:
        pack = pack.astype(F32)
        owners.append(pack[3:4, 0:nb])
        three = jnp.where(iota((4, pack.shape[1]), 0) < 3, pack[0:4], 0.0)
        point_rows += [three, jnp.zeros_like(three)]
        force_rows += [jnp.zeros_like(three), three]
    point_rows = jnp.concatenate(point_rows, axis=0).astype(BF16)
    force_rows = jnp.concatenate(force_rows, axis=0).astype(BF16)
    fields = (dot(point_rows, up_ref[...]) + dot(force_rows, bend_ref[...])).astype(BF16)
    fields = jnp.concatenate(
        [fields, jnp.zeros((8 * cells, tiles * TILE - fine), BF16)], axis=1
    )
    mix = interleave_matrix(blk)
    stacked = jnp.concatenate(
        [fields[:, t * TILE : (t + 1) * TILE] for t in range(tiles)], axis=0
    )
    parted = dot(stacked, mix)
    by_point = [
        jnp.concatenate(
            [
                parted[t * 8 * cells : (t + 1) * 8 * cells, k * group : (k + 1) * group]
                for t in range(tiles)
            ],
            axis=1,
        )[:, 0:nb]
        for k in range(blk)
    ]
    leaf_ids = iota((cells, nb), 0).astype(F32)
    chosen = jnp.concatenate([(leaf_ids == own).astype(F32) for own in owners], axis=0)
    earlier = (iota((nb, nb), 0) < iota((nb, nb), 1)).astype(BF16)
    before = dot(chosen.astype(BF16), earlier) * chosen
    spot_ids = iota((spots, nb), 0).astype(F32)
    sorts, by_leaf = [], []
    for c in range(cells):
        rank = jnp.sum(before[c * cells : (c + 1) * cells], axis=0, keepdims=True)
        sorts.append((spot_ids == owners[c] * capacity + rank).astype(BF16))
        rows = jnp.concatenate([by_point[k][8 * c : 8 * c + 8] for k in range(blk)], axis=0)
        by_leaf.append(dot_lanes(rows.astype(BF16), sorts[c]))
    farthest = jnp.max(
        sum(jnp.square(by_leaf[c][8 * k : 8 * k + 4]) for c in range(cells) for k in range(blk))
    )

    def all_leaves(sums):
        found = []
        for leaf in range(cells):
            rows = jnp.concatenate(
                [
                    by_leaf[c][8 * k : 8 * k + 8, leaf * capacity : (leaf + 1) * capacity]
                    for c in range(cells)
                    for k in range(blk)
                ],
                axis=1,
            )
            targets = rows[:, 0 : capacity * blk]
            upright = targets.T
            spread = [
                jnp.broadcast_to(upright[:, k : k + 1], (capacity * blk, 128)) for k in range(3)
            ]
            velocity = sums(spread, rows, targets) * STOKES_SCALE
            found.append(
                jnp.concatenate(
                    [velocity[:, k * capacity : (k + 1) * capacity] for k in range(blk)], axis=0
                )
            )
        found = jnp.concatenate(found, axis=1)
        high, low = split_bf16(found)
        back = dot(jnp.concatenate([high, low], axis=0), sorts[0])
        back = back[: 4 * blk] + back[4 * blk :]
        back = jnp.concatenate(
            [back, jnp.zeros((4 * blk, tiles * group - nb), F32)], axis=1
        )
        pieces = [
            jnp.concatenate(
                [back[4 * k : 4 * k + 4, t * group : (t + 1) * group] for k in range(blk)], axis=1
            )
            for t in range(tiles)
        ]
        high, low = split_bf16(jnp.concatenate(pieces, axis=0))
        natural = dot_lanes(high, mix) + dot_lanes(low, mix)
        for t in range(tiles):
            stop = min((t + 1) * TILE, fine)
            out_ref[0:4, t * TILE : stop] = natural[4 * t : 4 * t + 4, 0 : stop - t * TILE]

    small = farthest <= EXPAND_LIMIT
    pl.when(small)(functools.partial(all_leaves, expanded_sums))
    pl.when(jnp.logical_not(small))(functools.partial(all_leaves, direct_sums))


def far_kernel(blk, cells, regions, list_ref, packs_ref, near_ref, bend_ref, dens_ref, trans_ref, eval_ref, smooth_ref, out_ref):
    listed = list_ref.shape[1]
    fine = bend_ref.shape[1]
    nb = fine // blk
    points = eval_ref.shape[0]
    per_region = OCTANTS_PER_OWNER * cells
    rows = cells * 3 * listed
    devices = cells * regions
    row = iota((rows, 1), 0)
    entry, comp, cell = row % listed, row // listed % 3, row // (3 * listed)
    octant = jnp.zeros((rows, 1), jnp.int32)
    region = jnp.zeros((rows, 1), jnp.int32)
    for l in range(listed):
        wanted = list_ref[0, l]
        octant = jnp.where(entry == l, wanted % per_region, octant)
        region = jnp.where(entry == l, wanted // per_region, region)
    source = (cell * regions + region) * 4
    columns = iota((rows, devices * 4), 1)
    flat = packs_ref[...].reshape(devices * 4, packs_ref.shape[2])
    coarse = dot((columns == source + comp).astype(BF16), flat)
    marks = dot((columns == source + 3).astype(BF16), flat)
    inside = (marks[:, nb : 2 * nb] == octant.astype(F32)).astype(BF16)
    widen = (iota((nb, fine), 0) == iota((nb, fine), 1) // blk).astype(BF16)
    inside = dot(inside, widen)
    forces = dot(coarse.astype(BF16), bend_ref[...]).astype(BF16).astype(F32)
    density = dot_lanes((forces * inside).astype(BF16), dens_ref[...])
    span = 3 * listed
    density = sum(density[c * span : (c + 1) * span] for c in range(cells)).astype(BF16)
    expansion = sum(
        dot(density[k * listed : (k + 1) * listed], trans_ref[k * points : (k + 1) * points, :])
        for k in range(3)
    )
    far = jnp.sum(expansion.astype(BF16).astype(F32), axis=0, keepdims=True)
    far = jnp.concatenate(
        [far[:, k * points : (k + 1) * points] for k in range(3)] + [jnp.zeros((1, points), F32)],
        axis=0,
    )
    total = near_ref[0:4, :] + dot(far.astype(BF16), eval_ref[...])
    velocity = dot_lanes(total.astype(BF16), smooth_ref[...])
    for k in range(3):
        out_ref[k] = velocity[k : k + 1]


def vmem(megabytes):
    return pltpu.CompilerParams(vmem_limit_bytes=megabytes << 20)


def on_device(
    cell_shape,
    upsample,
    bending,
    to_density,
    translate,
    evaluate,
    smoothing,
    block_owner,
    block_octant,
    far_list,
):
    cells, regions = lax.axis_size("cells"), lax.axis_size("region")
    coarse, fine = upsample.shape
    nb = block_owner.shape[0]
    blk = fine // nb
    pack, spread = pl.pallas_call(
        pack_kernel,
        out_shape=(
            jax.ShapeDtypeStruct((4, coarse), BF16),
            jax.ShapeDtypeStruct((cells * regions, 4, coarse), BF16),
        ),
        name="pack",
    )(cell_shape.reshape(3, coarse), block_owner.reshape(1, nb), block_octant.reshape(1, nb))
    others = [
        lax.ppermute(pack, "cells", [(i, i ^ k) for i in range(cells)])
        for k in sorted(range(1, cells), reverse=True)
    ]
    everyone = lax.all_to_all(spread, ("cells", "region"), split_axis=0, concat_axis=0, tiled=True)
    near = pl.pallas_call(
        functools.partial(near_kernel, blk),
        out_shape=jax.ShapeDtypeStruct((4, fine), F32),
        compiler_params=vmem(32),
        cost_estimate=pl.CostEstimate(flops=5 * 10**9, bytes_accessed=10**6, transcendentals=0),
        name="near",
    )(pack, *others, upsample, bending)
    in_vmem = pl.BlockSpec(memory_space=pltpu.VMEM)
    velocity = pl.pallas_call(
        functools.partial(far_kernel, blk, cells, regions),
        out_shape=jax.ShapeDtypeStruct((3, 1, coarse), F32),
        in_specs=[pl.BlockSpec(memory_space=pltpu.SMEM)] + [in_vmem] * 7,
        compiler_params=vmem(32),
        name="far",
    )(far_list, everyone, near, bending, to_density.T, translate, evaluate, smoothing.T)
    return velocity.transpose(1, 0, 2)


def solution(mesh):
    own = P(("cells", "region"))
    return jax.shard_map(
        on_device,
        mesh=mesh,
        in_specs=(own, P(), P(), P(), P(), P(), P(), own, own, own),
        out_specs=own,
        check_vma=False,
    )
```

time: 100 us -> 37.2 us (0.37)
  blocking collectives: 30.7 us -> 0 us
  other arithmetic: 30.1 us -> 0 us
  Pallas kernels: 0 us -> 16.8 us
  local copies, waits for them, and re-layouts: 17.9 us -> 9.05 us
  matrix products: 7.63 us -> 0 us
  waiting for transfers between devices: 4.64 us -> 0.01 us
  starting transfers between devices: 8.43 us -> 10.8 us
    reduce_sum x11 -> x0, other arithmetic: 26.7 us -> none  [the longest x9 26.6 us: stokeslet(): vel_x = jnp.sum(direct * strength[0][None, :] + diff_x * radial, axis=1)]
    pallas_call x0 -> x3, Pallas kernels: none -> 16.8 us  [the longest x1 11.4 us: on_device(): pl.pallas_call(functools.partial(near_kernel, blk), out_shape=jax.ShapeDt...]
    psum x1 -> x0, blocking collectives: 16.5 us -> none  [on_device(): summed = lax.psum(density_part, 'cells')]
    all_gather x1 -> x0, blocking collectives: 14.2 us -> none  [on_device(): lax.all_gather(expansion, 'region', axis=0, tiled=True)]
    scatter x1 -> x0, local copies, waits for them, and re-layouts: 8.62 us -> none  [on_device(): jnp.zeros((owners_count * capacity, 6, BLK), jnp.bfloat16).at[slot_index]]
    unnamed x11 -> x18, local copies, waits for them, and re-layouts: 0.03 us -> 7.8 us
    dot_general x6 -> x0, matrix products: 7.63 us -> none  [the longest x1 2.76 us: on_device(): jnp.dot(total.reshape(cell_count * 3, P_FINE), smoothing, preferred_eleme...]
    all_to_all x2 -> x1, waiting for transfers between devices: 4.64 us -> 0.01 us  [on_device(): lax.all_to_all(spread, ('cells', 'region'), split_axis=0, concat_axis=0,...]
  transfers between devices with their start and end apart: 2 -> 4, of which waited for: 1 -> 0; matrix products, arithmetic and copies ran while one was open for 2% -> 0% of each run, Pallas kernels for 0% -> 31%
where the time goes in v1:
time: 37.2 us; the launch traced here: 36.7 us
  Pallas kernels  16.8 us (45%)
  starting transfers between devices  10.8 us (29%)
  local copies, waits for them, and re-layouts  9.05 us (24%)
    pallas_call x1, Pallas kernels, on_device(): pl.pallas_call(functools.partial(near_kernel, blk), out_shape=jax.ShapeDt...  11.4 us
    unnamed x18, local copies, waits for them, and re-layouts  7.8 us
    all_to_all x1, starting transfers between devices, on_device(): lax.all_to_all(spread, ('cells', 'region'), split_axis=0, concat_axis=0,...  6.32 us
    ppermute x3, starting transfers between devices, on_device(): lax.ppermute(pack, 'cells', [(i, i ^ k) for i in range(cells)])  4.46 us
    pallas_call x1, Pallas kernels, on_device(): pl.pallas_call(functools.partial(far_kernel, blk, cells, regions), out_sh...  3.92 us
    pallas_call x1, Pallas kernels, on_device(): pl.pallas_call(pack_kernel, out_shape=(jax.ShapeDtypeStruct((4, coarse),...  1.47 us
    reshape x1, local copies, waits for them, and re-layouts, on_device(): block_octant.reshape(1, nb)  1.24 us
  transfers between devices with their start and end apart: 4, of which 0 were waited for; matrix products, arithmetic and copies ran while one was open for 0% of the time, Pallas kernels for 31%

profile of v1, /device:TPU:0, one launch (start us, length us, event | category | flops | bytes accessed | tf_op | source)
XLA Modules:
  0.0 36.7 jit_solution(11904327367347654433)
XLA Ops:
  0.0 1.2 %reshape.11.octant_ref = s32[1,264]{1,0:T(1,128)} reshape(s32[264]{0:T(512)} %param.18) | data formatting | bytes 2112 | tf_op jit(solution)/shard_map/reshape | solution.py:311
  1.2 1.5 %pack.1 = (bf16[4,544]{1,0:T(4,128)(2,1)}, bf16[32,4,544]{2,1,0:T(4,128)(2,1)}) custom-call(bf16[3,544]{1,0:T(4,128)(2,1)} %bitcast.7, s32[1,264]{1,0:T(1,128)} %bitcast.8, s32[1,264]{1,0:T(1,128)} %reshape.11.octant_ref), custom_call_target="tpu_custom_call" | custom-call | tf_op jit(solution)/shard_map/pack/pallas_call | solution.py:304
  2.7 2.9 %collective-permute-start.2 = (bf16[4,544]{1,0:T(4,128)(2,1)}, bf16[4,544]{1,0:T(4,128)(2,1)S(1)}, u32[]{:S(2)}, u32[]{:S(2)}) collective-permute-start(bf16[4,544]{1,0:T(4,128)(2,1)} %get-tuple-element.8.refs_0_), channel_id=1, source_target_pairs={{0,8},{8,0},{16,24},{24,16},{1,9},{9,1},{17,25},{25,17},{2,10},{10... | collective-permute-start | bytes 13064 | tf_op jit(solution)/shard_map/ppermute | solution.py:313
  5.7 1.5 %collective-permute-start.1 = (bf16[4,544]{1,0:T(4,128)(2,1)}, bf16[4,544]{1,0:T(4,128)(2,1)S(1)}, u32[]{:S(2)}, u32[]{:S(2)}) collective-permute-start(bf16[4,544]{1,0:T(4,128)(2,1)} %get-tuple-element.8.refs_0_), channel_id=1, source_target_pairs={{0,16},{8,24},{16,0},{24,8},{1,17},{9,25},{17,1},{25,9},{2,18},{10... | collective-permute-start | bytes 13064 | tf_op jit(solution)/shard_map/ppermute | solution.py:313
  7.2 0.0 collective-permute-start
  7.2 0.0 copy-start.6
  7.2 6.3 %all-to-all-start = ((bf16[32,4,544]{2,1,0:T(4,128)(2,1)}), bf16[32,4,544]{2,1,0:T(4,128)(2,1)S(1)}, u32[]{:S(2)}, u32[]{:S(2)}) async-start(bf16[32,4,544]{2,1,0:T(4,128)(2,1)} %get-tuple-element.7), calls=%async_computation | async-start | bytes 327680 | tf_op jit(solution)/shard_map/all_to_all | solution.py:316
  13.5 0.0 collective-permute-done.2.refs_3_
  13.5 0.0 collective-permute-done.1.refs_2_
  13.5 0.0 collective-permute-done.refs_1_
  13.5 0.0 copy-start
  13.6 1.7 %copy-done = bf16[544,2112]{1,0:T(8,128)(2,1)S(1)} copy-done((bf16[544,2112]{1,0:T(8,128)(2,1)S(1)}, bf16[544,2112]{1,0:T(8,128)(2,1)}, u32[]{:S(2)}) %copy-start) | copy-done | bytes 2297880
  15.2 0.0 copy-start.7
  15.2 1.7 %copy-done.7 = bf16[544,2112]{1,0:T(8,128)(2,1)S(1)} copy-done((bf16[544,2112]{1,0:T(8,128)(2,1)S(1)}, bf16[544,2112]{1,0:T(8,128)(2,1)}, u32[]{:S(2)}) %copy-start.7) | copy-done | bytes 2297880
  16.9 0.0 copy-start.8
  16.9 0.7 %copy-done.8 = bf16[4,544]{1,0:T(4,128)(2,1)S(1)} copy-done((bf16[4,544]{1,0:T(4,128)(2,1)S(1)}, bf16[4,544]{1,0:T(4,128)(2,1)}, u32[]{:S(2)}) %copy-start.8) | copy-done | bytes 4376
  17.6 0.0 copy-start.1
  17.6 0.0 copy-start.3
  17.6 11.4 %near.1.near_ref = f32[4,2112]{1,0:T(4,128)S(1)} custom-call(bf16[4,544]{1,0:T(4,128)(2,1)S(1)} %copy-done.8, bf16[4,544]{1,0:T(4,128)(2,1)S(1)} %collective-permute-done.refs_1_, bf16[4,544]{1,0:T(4,128)(2,1)S(1)} %collective-permute-done.1.refs_2_, bf16[4,544]{1,0:T(4,128)(2,1)S(1)} %collective-permute-done.2.refs_3_, bf16[544,2112]{1,0:T(8,128)(2,1)S(1)} %copy-done.7, ...), custom_call_target="tpu_custom_call" | custom-call | flops 5000000000 | bytes 1000000 | tf_op jit(solution)/shard_map/near/pallas_call | solution.py:317
  29.0 0.0 all-to-all-done.packs_ref
  29.0 0.0 copy-done.6
  29.0 0.0 copy-done.1
  29.0 0.0 copy-done.3
  29.0 0.0 copy-start.2
  29.0 1.7 %copy-done.2 = bf16[2112,544]{0,1:T(8,128)(2,1)S(1)} copy-done((bf16[2112,544]{0,1:T(8,128)(2,1)S(1)}, bf16[2112,544]{0,1:T(8,128)(2,1)}, u32[]{:S(2)}) %copy-start.2) | copy-done | bytes 2297880
  30.7 0.0 copy-start.4
  30.7 1.1 %copy-done.4 = bf16[152,2112]{1,0:T(8,128)(2,1)S(1)} copy-done((bf16[152,2112]{1,0:T(8,128)(2,1)S(1)}, bf16[152,2112]{1,0:T(8,128)(2,1)}, u32[]{:S(2)}) %copy-start.4) | copy-done | bytes 642072
  31.8 0.0 copy-start.5
  31.8 1.0 %copy-done.5 = bf16[456,456]{1,0:T(8,128)(2,1)S(1)} copy-done((bf16[456,456]{1,0:T(8,128)(2,1)S(1)}, bf16[456,456]{1,0:T(8,128)(2,1)}, u32[]{:S(2)}) %copy-start.5) | copy-done | bytes 415896
  32.8 3.9 %far.1 = f32[3,1,544]{2,1,0:T(1,128)} custom-call(s32[1,8]{1,0:T(1,128)S(1)} %copy-done.6, bf16[32,4,544]{2,1,0:T(4,128)(2,1)S(1)} %all-to-all-done.packs_ref, f32[4,2112]{1,0:T(4,128)S(1)} %near.1.near_ref, bf16[544,2112]{1,0:T(8,128)(2,1)S(1)} %copy-done.1, bf16[152,2112]{1,0:T(8,128)(2,1)S(1)} %bitcast.6, bf16[456,456]{1,0:T(8,128)(2,1)S(1)} %copy-done.5, ...), custom_call_target="tpu_custom_call" | custom-call | tf_op jit(solution)/shard_map/far/pallas_call | solution.py:325
Async XLA Ops:
  2.7 10.8 %collective-permute-start.2 = (bf16[4,544]{1,0:T(4,128)(2,1)}, bf16[4,544]{1,0:T(4,128)(2,1)S(1)}, u32[]{:S(2)}, u32[]{:S(2)}) collective-permute-start(bf16[4,544]{1,0:T(4,128)(2,1)} %get-tuple-element.8.refs_0_), channel_id=1, source_target_pairs={{0,8},{8,0},{16,24},{24,16},{1,9},{9,1},{17,25},{25,17},{2,10},{10... | collective-permute-start | bytes 13064 | tf_op jit(solution)/shard_map/ppermute | solution.py:313
  5.7 7.9 %collective-permute-start.1 = (bf16[4,544]{1,0:T(4,128)(2,1)}, bf16[4,544]{1,0:T(4,128)(2,1)S(1)}, u32[]{:S(2)}, u32[]{:S(2)}) collective-permute-start(bf16[4,544]{1,0:T(4,128)(2,1)} %get-tuple-element.8.refs_0_), channel_id=1, source_target_pairs={{0,16},{8,24},{16,0},{24,8},{1,17},{9,25},{17,1},{25,9},{2,18},{10... | collective-permute-start | bytes 13064 | tf_op jit(solution)/shard_map/ppermute | solution.py:313
  7.2 6.4 %collective-permute-start = (bf16[4,544]{1,0:T(4,128)(2,1)}, bf16[4,544]{1,0:T(4,128)(2,1)S(1)}, u32[]{:S(2)}, u32[]{:S(2)}) collective-permute-start(bf16[4,544]{1,0:T(4,128)(2,1)} %get-tuple-element.8.refs_0_), channel_id=1, source_target_pairs={{0,24},{8,16},{16,8},{24,0},{1,25},{9,17},{17,9},{25,1},{2,26},{10... | collective-permute-start | bytes 13064 | tf_op jit(solution)/shard_map/ppermute | solution.py:313
  7.2 21.8 %copy-start.6 = (s32[1,8]{1,0:T(1,128)S(1)}, s32[1,8]{1,0:T(1,128)}, u32[]{:S(2)}) copy-start(s32[1,8]{1,0:T(1,128)} %list_ref.1) | copy-start | bytes 100
  7.2 21.8 %all-to-all-start = ((bf16[32,4,544]{2,1,0:T(4,128)(2,1)}), bf16[32,4,544]{2,1,0:T(4,128)(2,1)S(1)}, u32[]{:S(2)}, u32[]{:S(2)}) async-start(bf16[32,4,544]{2,1,0:T(4,128)(2,1)} %get-tuple-element.7), calls=%async_computation | async-start | bytes 327680 | tf_op jit(solution)/shard_map/all_to_all | solution.py:316
  13.5 1.7 %copy-start = (bf16[544,2112]{1,0:T(8,128)(2,1)S(1)}, bf16[544,2112]{1,0:T(8,128)(2,1)}, u32[]{:S(2)}) copy-start(bf16[544,2112]{1,0:T(8,128)(2,1)} %bend_ref.1) | copy-start | bytes 6893572
  15.2 1.7 %copy-start.7 = (bf16[544,2112]{1,0:T(8,128)(2,1)S(1)}, bf16[544,2112]{1,0:T(8,128)(2,1)}, u32[]{:S(2)}) copy-start(bf16[544,2112]{1,0:T(8,128)(2,1)} %refs_4_.1) | copy-start | bytes 6893572
  16.9 0.7 %copy-start.8 = (bf16[4,544]{1,0:T(4,128)(2,1)S(1)}, bf16[4,544]{1,0:T(4,128)(2,1)}, u32[]{:S(2)}) copy-start(bf16[4,544]{1,0:T(4,128)(2,1)} %get-tuple-element.8.refs_0_) | copy-start | bytes 13060
  17.6 11.4 %copy-start.1 = (bf16[544,2112]{1,0:T(8,128)(2,1)S(1)}, bf16[544,2112]{1,0:T(8,128)(2,1)}, u32[]{:S(2)}) copy-start(bf16[544,2112]{1,0:T(8,128)(2,1)} %bend_ref.1) | copy-start | bytes 6893572
  17.6 11.4 %copy-start.3 = (bf16[2112,152]{0,1:T(8,128)(2,1)S(1)}, bf16[2112,152]{0,1:T(8,128)(2,1)}, u32[]{:S(2)}) copy-start(bf16[2112,152]{0,1:T(8,128)(2,1)} %param.13) | copy-start | bytes 1926148
  29.0 1.7 %copy-start.2 = (bf16[2112,544]{0,1:T(8,128)(2,1)S(1)}, bf16[2112,544]{0,1:T(8,128)(2,1)}, u32[]{:S(2)}) copy-start(bf16[2112,544]{0,1:T(8,128)(2,1)} %param.16) | copy-start | bytes 6893572
  30.7 1.1 %copy-start.4 = (bf16[152,2112]{1,0:T(8,128)(2,1)S(1)}, bf16[152,2112]{1,0:T(8,128)(2,1)}, u32[]{:S(2)}) copy-start(bf16[152,2112]{1,0:T(8,128)(2,1)} %eval_ref.1) | copy-start | bytes 1926148
  31.8 1.0 %copy-start.5 = (bf16[456,456]{1,0:T(8,128)(2,1)S(1)}, bf16[456,456]{1,0:T(8,128)(2,1)}, u32[]{:S(2)}) copy-start(bf16[456,456]{1,0:T(8,128)(2,1)} %trans_ref.1) | copy-start | bytes 1247620

commit v2 on v1

v2 whole, which is shorter than its diff:
```python
import functools

import jax
import jax.numpy as jnp
from jax import lax
from jax.experimental import pallas as pl
from jax.experimental.pallas import tpu as pltpu
from jax.sharding import PartitionSpec as P

EPSILON_SQ = 0.0625
STOKES_SCALE = 1.0 / (8.0 * 3.141592653589793)
EXPAND_LIMIT = 128.0
TILE = 256
OCTANTS_PER_OWNER = 2
F32 = jnp.float32
BF16 = jnp.bfloat16
LANES = (((1,), (1,)), ((), ()))


def iota(shape, dim):
    return lax.broadcasted_iota(jnp.int32, shape, dim)


def dot(a, b):
    return jnp.dot(a, b, preferred_element_type=F32)


def dot_lanes(a, b):
    return lax.dot_general(a, b, LANES, preferred_element_type=F32)


def split_bf16(x):
    high = x.astype(BF16)
    return high, (x - high.astype(F32)).astype(BF16)


def row_chunks(rows):
    return [(start, min(start + TILE, rows)) for start in range(0, rows, TILE)]


class Arriving:
    def __init__(self, sources, targets, sems):
        self.targets = targets
        self.pieces = [
            [
                (pltpu.make_async_copy(src.at[a:b], dst.at[a:b], sems.at[n, i]), a, b)
                for i, (a, b) in enumerate(row_chunks(src.shape[0]))
            ]
            for n, (src, dst) in enumerate(zip(sources, targets))
        ]

    def start(self, n):
        for copy, _, _ in self.pieces[n]:
            copy.start()

    def wait(self, n):
        for copy, _, _ in self.pieces[n]:
            copy.wait()

    def dot(self, lhs, n):
        total = None
        for copy, a, b in self.pieces[n]:
            copy.wait()
            part = dot(lhs[:, a:b], self.targets[n][a:b, :])
            total = part if total is None else total + part
        return total


def pack_kernel(cell_ref, owner_ref, octant_ref, pack_ref, spread_ref):
    nb = owner_ref.shape[1]
    width = cell_ref.shape[1]
    octant = octant_ref[...].reshape(1, nb)
    pack_ref[0:3, :] = cell_ref[...]
    row = jnp.concatenate(
        [
            owner_ref[...].astype(F32),
            octant.astype(F32),
            jnp.zeros((1, width - 2 * nb), F32),
        ],
        axis=1,
    )
    pack_ref[3:4, :] = row.astype(BF16)
    spread_ref[...] = jnp.broadcast_to(pack_ref[...][None], spread_ref.shape)


def interleave_matrix(blk):
    group = TILE // blk
    point, lane = iota((TILE, TILE), 0), iota((TILE, TILE), 1)
    return ((point % blk == lane // group) & (point // blk == lane % group)).astype(BF16)


def source_columns(rows):
    forces = jnp.concatenate([rows[4:8], rows[4:8]], axis=0)
    places = jnp.concatenate([rows[0:4], rows[0:4]], axis=0)
    upper = iota(rows.shape, 0) < 4
    groups = []
    square = jnp.zeros_like(rows)
    inner = jnp.zeros_like(rows)
    for k in range(3):
        x_k = jnp.broadcast_to(rows[k : k + 1], rows.shape)
        product = x_k * forces
        high = product.astype(BF16).astype(F32)
        groups.append(jnp.where(upper, high, product - high))
        square = square + x_k * x_k
        inner = inner + x_k * rows[4 + k : 5 + k]
    rest = square * forces + inner * places
    high = rest.astype(BF16).astype(F32)
    middle = (rest - high).astype(BF16).astype(F32)
    groups.append(jnp.where(upper, high, middle))
    groups.append(jnp.where(upper, rest - high - middle, forces))
    return jnp.concatenate(groups, axis=0).astype(BF16)


def three_parts(x):
    high = x.astype(BF16).astype(F32)
    middle = (x - high).astype(BF16).astype(F32)
    return high, middle, x - high - middle


def distance_factors(rows, targets):
    def side(points, scale, extra, squares_first):
        square = jnp.sum(jnp.square(points[0:4]), axis=0, keepdims=True) + extra
        ones = [jnp.ones_like(square)] * 3
        squares = list(three_parts(square))
        parts = squares + ones if squares_first else ones + squares
        unused = jnp.zeros((7, points.shape[1]), F32)
        return jnp.concatenate([points[0:3] * scale] + parts + [unused], axis=0)

    source = side(rows, -2.0, 0.0, False).astype(BF16)
    target = side(targets, 1.0, EPSILON_SQ, True).T.astype(BF16)
    return source, target


def expanded_sums(rows, targets):
    columns = source_columns(rows)
    source, target = distance_factors(rows, targets)
    inverse = lax.rsqrt(dot(target, source))
    cubed = (inverse * inverse * inverse).astype(BF16)
    sums = dot_lanes(columns, cubed)
    place = targets[0:4]
    moment = [sums[8 * k : 8 * k + 4] + sums[8 * k + 4 : 8 * k + 8] for k in range(3)]
    rest = sums[24:28] + sums[28:32] + sums[32:36]
    force = sums[36:40]
    square = jnp.sum(place * place, axis=0, keepdims=True)
    along = jnp.sum(place * force, axis=0, keepdims=True)
    trace = moment[0][0:1] + moment[1][1:2] + moment[2][2:3]
    cross = [jnp.sum(place * moment[k], axis=0, keepdims=True) for k in range(3)]
    cross = jnp.concatenate(cross + [jnp.zeros_like(trace)], axis=0)
    weighted = place[0:1] * moment[0] + place[1:2] * moment[1] + place[2:3] * moment[2]
    return (
        (square + 2.0 * EPSILON_SQ) * force + rest - 2.0 * weighted + place * (along - trace) - cross
    )


def direct_sums(rows, targets):
    strength = rows[4:8].astype(BF16)
    ones = jnp.ones((1, rows.shape[1]), F32)
    places = jnp.concatenate([rows[0:3], ones], axis=0).astype(BF16)
    upright = targets.T
    sums = None
    for start in range(0, rows.shape[1], TILE):
        stop = min(start + TILE, rows.shape[1])
        diffs = [upright[:, k : k + 1] - rows[k : k + 1, start:stop] for k in range(3)]
        dist = diffs[0] * diffs[0] + diffs[1] * diffs[1] + diffs[2] * diffs[2] + EPSILON_SQ
        inverse = lax.rsqrt(dist)
        cubed = inverse * inverse * inverse
        direct = ((dist + EPSILON_SQ) * cubed).astype(BF16)
        along = sum(diffs[k] * rows[4 + k : 5 + k, start:stop] for k in range(3))
        radial = (along * cubed).astype(BF16)
        near = dot_lanes(strength[:, start:stop], direct)
        away = dot_lanes(places[:, start:stop], radial)
        part = jnp.concatenate([near, away], axis=0)
        sums = part if sums is None else sums + part
    return sums[0:4] + targets[0:4] * sums[7:8] - sums[4:8]


def near_kernel(blk, packs_given, *refs):
    cell_ref, owner_ref, *pack_refs = refs[: packs_given + 2]
    bend_ref, up_hbm, out_ref, up_ref, rows_ref, found_ref, sems = refs[packs_given + 2 :]
    arriving = Arriving([up_hbm], [up_ref], sems)
    arriving.start(0)
    packs = [ref[...].astype(F32) for ref in pack_refs]
    cells = len(packs) + 1
    fine = up_ref.shape[1]
    nb = fine // blk
    capacity = nb // cells + 2
    spots = cells * capacity
    group = TILE // blk
    tiles = -(-fine // TILE)
    point_rows, force_rows = [], []
    coarse = [jnp.concatenate([cell_ref[...].astype(F32), jnp.zeros((1, cell_ref.shape[1]), F32)], axis=0)]
    coarse += [jnp.where(iota(pack.shape, 0) < 3, pack, 0.0) for pack in packs]
    owners = [owner_ref[...].astype(F32)] + [pack[3:4, 0:nb] for pack in packs]
    for three in coarse:
        point_rows += [three, jnp.zeros_like(three)]
        force_rows += [jnp.zeros_like(three), three]
    point_rows = jnp.concatenate(point_rows, axis=0).astype(BF16)
    force_rows = jnp.concatenate(force_rows, axis=0).astype(BF16)
    leaf_ids = iota((cells, nb), 0).astype(F32)
    chosen = jnp.concatenate([(leaf_ids == own).astype(F32) for own in owners], axis=0)
    earlier = (iota((nb, nb), 0) < iota((nb, nb), 1)).astype(BF16)
    before = dot(chosen.astype(BF16), earlier) * chosen
    spot_ids = iota((spots, nb), 0).astype(F32)
    sorts = []
    for c in range(cells):
        rank = jnp.sum(before[c * cells : (c + 1) * cells], axis=0, keepdims=True)
        sorts.append((spot_ids == owners[c] * capacity + rank).astype(BF16))
    mix = interleave_matrix(blk)
    fields = (dot(force_rows, bend_ref[...]) + arriving.dot(point_rows, 0)).astype(BF16)
    fields = jnp.concatenate(
        [fields, jnp.zeros((8 * cells, tiles * TILE - fine), BF16)], axis=1
    )
    stacked = jnp.concatenate(
        [fields[:, t * TILE : (t + 1) * TILE] for t in range(tiles)], axis=0
    )
    parted = dot(stacked, mix)
    by_point = [
        jnp.concatenate(
            [
                parted[t * 8 * cells : (t + 1) * 8 * cells, k * group : (k + 1) * group]
                for t in range(tiles)
            ],
            axis=1,
        )[:, 0:nb]
        for k in range(blk)
    ]
    by_leaf = []
    for c in range(cells):
        rows = jnp.concatenate([by_point[k][8 * c : 8 * c + 8] for k in range(blk)], axis=0)
        by_leaf.append(dot_lanes(rows.astype(BF16), sorts[c]))
    for leaf in range(cells):
        rows_ref[leaf] = jnp.concatenate(
            [
                by_leaf[c][8 * k : 8 * k + 8, leaf * capacity : (leaf + 1) * capacity]
                for c in range(cells)
                for k in range(blk)
            ],
            axis=1,
        )
    farthest = jnp.max(
        sum(jnp.square(by_leaf[c][8 * k : 8 * k + 4]) for c in range(cells) for k in range(blk))
    )

    def each_leaf(sums, leaf, _):
        rows = rows_ref[leaf]
        velocity = sums(rows, rows[:, 0 : capacity * blk]) * STOKES_SCALE
        found_ref[leaf] = jnp.concatenate(
            [velocity[:, k * capacity : (k + 1) * capacity] for k in range(blk)], axis=0
        )
        return 0

    lax.fori_loop(0, cells, functools.partial(each_leaf, expanded_sums), 0, unroll=cells <= 4)

    @pl.when(farthest > EXPAND_LIMIT)
    def _():
        lax.fori_loop(0, cells, functools.partial(each_leaf, direct_sums), 0)

    found = jnp.concatenate([found_ref[leaf] for leaf in range(cells)], axis=1)
    high, low = split_bf16(found)
    back = dot(jnp.concatenate([high, low], axis=0), sorts[0])
    back = back[: 4 * blk] + back[4 * blk :]
    back = jnp.concatenate([back, jnp.zeros((4 * blk, tiles * group - nb), F32)], axis=1)
    pieces = [
        jnp.concatenate(
            [back[4 * k : 4 * k + 4, t * group : (t + 1) * group] for k in range(blk)], axis=1
        )
        for t in range(tiles)
    ]
    high, low = split_bf16(jnp.concatenate(pieces, axis=0))
    natural = dot_lanes(high, mix) + dot_lanes(low, mix)
    for t in range(tiles):
        stop = min((t + 1) * TILE, fine)
        out_ref[0:4, t * TILE : stop] = natural[4 * t : 4 * t + 4, 0 : stop - t * TILE]

def far_kernel(blk, cells, regions, *refs):
    list_ref, packs_ref, near_ref, bend_ref, *in_hbm = refs[:8]
    out_ref, *in_vmem, sems = refs[8:]
    dens_ref, trans_ref, eval_ref, smooth_ref = in_vmem
    arriving = Arriving(in_hbm, in_vmem, sems)
    for n in range(len(in_hbm)):
        arriving.start(n)
    listed = list_ref.shape[1]
    fine = bend_ref.shape[1]
    nb = fine // blk
    points = eval_ref.shape[0]
    per_region = OCTANTS_PER_OWNER * cells
    rows = cells * 3 * listed
    devices = cells * regions
    row = iota((rows, 1), 0)
    entry, comp, cell = row % listed, row // listed % 3, row // (3 * listed)
    octant = jnp.zeros((rows, 1), jnp.int32)
    region = jnp.zeros((rows, 1), jnp.int32)
    for l in range(listed):
        wanted = list_ref[0, l]
        octant = jnp.where(entry == l, wanted % per_region, octant)
        region = jnp.where(entry == l, wanted // per_region, region)
    source = (cell * regions + region) * 4
    columns = iota((rows, devices * 4), 1)
    flat = packs_ref[...].reshape(devices * 4, packs_ref.shape[2])
    coarse = dot((columns == source + comp).astype(BF16), flat)
    marks = dot((columns == source + 3).astype(BF16), flat)
    inside = (marks[:, nb : 2 * nb] == octant.astype(F32)).astype(BF16)
    widen = (iota((nb, fine), 0) == iota((nb, fine), 1) // blk).astype(BF16)
    inside = dot(inside, widen)
    forces = dot(coarse.astype(BF16), bend_ref[...]).astype(BF16).astype(F32)
    arriving.wait(0)
    density = dot_lanes((forces * inside).astype(BF16), dens_ref[...])
    span = 3 * listed
    density = sum(density[c * span : (c + 1) * span] for c in range(cells)).astype(BF16)
    arriving.wait(1)
    expansion = sum(
        dot(density[k * listed : (k + 1) * listed], trans_ref[k * points : (k + 1) * points, :])
        for k in range(3)
    )
    far = jnp.sum(expansion.astype(BF16).astype(F32), axis=0, keepdims=True)
    far = jnp.concatenate(
        [far[:, k * points : (k + 1) * points] for k in range(3)] + [jnp.zeros((1, points), F32)],
        axis=0,
    )
    arriving.wait(2)
    total = near_ref[0:4, :] + dot(far.astype(BF16), eval_ref[...])
    arriving.wait(3)
    velocity = dot_lanes(total.astype(BF16), smooth_ref[...])
    for k in range(3):
        out_ref[k] = velocity[k : k + 1]


def in_place(x):
    return pltpu.with_memory_space_constraint(x, pltpu.HBM)


def vmem(megabytes):
    return pltpu.CompilerParams(vmem_limit_bytes=megabytes << 20)


def on_device(
    cell_shape,
    upsample,
    bending,
    to_density,
    translate,
    evaluate,
    smoothing,
    block_owner,
    block_octant,
    far_list,
):
    cells, regions = lax.axis_size("cells"), lax.axis_size("region")
    coarse, fine = upsample.shape
    nb = block_owner.shape[0]
    blk = fine // nb
    own_cell, own_blocks = cell_shape.reshape(3, coarse), block_owner.reshape(1, nb)
    pack, spread = pl.pallas_call(
        pack_kernel,
        out_shape=(
            jax.ShapeDtypeStruct((4, coarse), BF16),
            jax.ShapeDtypeStruct((cells * regions, 4, coarse), BF16),
        ),
        cost_estimate=pl.CostEstimate(flops=5 * 10**10, bytes_accessed=10**6, transcendentals=0),
        name="pack",
    )(own_cell, own_blocks, block_octant)
    others = [
        lax.ppermute(pack, "cells", [(i, i ^ k) for i in range(cells)])
        for k in sorted(range(1, cells), reverse=True)
    ]
    everyone = lax.all_to_all(spread, ("cells", "region"), split_axis=0, concat_axis=0, tiled=True)
    in_vmem = pl.BlockSpec(memory_space=pltpu.VMEM)
    in_hbm = pl.BlockSpec(memory_space=pltpu.HBM)
    points = cells * (nb // cells + 2) * blk
    near = pl.pallas_call(
        functools.partial(near_kernel, blk, len(others)),
        out_shape=jax.ShapeDtypeStruct((4, fine), F32),
        in_specs=[in_vmem] * (cells + 2) + [in_hbm],
        scratch_shapes=[
            pltpu.VMEM(upsample.shape, BF16),
            pltpu.VMEM((cells, 8, points), F32),
            pltpu.VMEM((cells, 4 * blk, points // (cells * blk)), F32),
            pltpu.SemaphoreType.DMA((1, len(row_chunks(coarse)))),
        ],
        compiler_params=vmem(40),
        cost_estimate=pl.CostEstimate(flops=5 * 10**10, bytes_accessed=10**6, transcendentals=0),
        name="near",
    )(own_cell, own_blocks, *others, bending, in_place(upsample))
    later = [in_place(x) for x in (to_density.T, translate, evaluate, smoothing.T)]
    velocity = pl.pallas_call(
        functools.partial(far_kernel, blk, cells, regions),
        out_shape=jax.ShapeDtypeStruct((3, 1, coarse), F32),
        in_specs=[pl.BlockSpec(memory_space=pltpu.SMEM)] + [in_vmem] * 3 + [in_hbm] * 4,
        scratch_shapes=[pltpu.VMEM(x.shape, BF16) for x in later]
        + [pltpu.SemaphoreType.DMA((4, len(row_chunks(coarse))))],
        compiler_params=vmem(32),
        name="far",
    )(far_list, everyone, near, bending, *later)
    return velocity.transpose(1, 0, 2)


def solution(mesh):
    own = P(("cells", "region"))
    return jax.shard_map(
        on_device,
        mesh=mesh,
        in_specs=(own, P(), P(), P(), P(), P(), P(), own, own, own),
        out_specs=own,
        check_vma=False,
    )
```

time: 37.2 us -> 42.5 us (1.14)
  the two profiles are of different devices: /device:TPU:0 before, /device:TPU:1 now
where the time goes in v2:
time: 42.5 us; the launch traced here: 42.1 us
  Pallas kernels  31.4 us (74%)
  starting transfers between devices  10.6 us (25%)
    pallas_call x1, Pallas kernels, on_device(): pl.pallas_call(functools.partial(near_kernel, blk, len(others)), out_shap...  24.6 us
    all_to_all x1, starting transfers between devices, on_device(): lax.all_to_all(spread, ('cells', 'region'), split_axis=0, concat_axis=0,...  7.3 us
    pallas_call x1, Pallas kernels, on_device(): pl.pallas_call(functools.partial(far_kernel, blk, cells, regions), out_sh...  5.26 us
    ppermute x3, starting transfers between devices, on_device(): lax.ppermute(pack, 'cells', [(i, i ^ k) for i in range(cells)])  3.28 us
    pallas_call x1, Pallas kernels, on_device(): pl.pallas_call(pack_kernel, out_shape=(jax.ShapeDtypeStruct((4, coarse),...  1.62 us
  transfers between devices with their start and end apart: 4, of which 0 were waited for; matrix products, arithmetic and copies ran while one was open for 0% of the time, Pallas kernels for 58%

profile of v2, /device:TPU:1, one launch (start us, length us, event | category | flops | bytes accessed | tf_op | source)
XLA Modules:
  0.0 42.1 jit_solution(12281592190449951976)
XLA Ops:
  0.0 0.0 copy-start
  0.0 0.0 copy-start.2
  0.0 0.0 copy-start.3
  0.0 1.6 %pack.1 = (bf16[4,544]{1,0:T(4,128)(2,1)}, bf16[32,4,544]{2,1,0:T(4,128)(2,1)}) custom-call(bf16[3,544]{1,0:T(4,128)(2,1)} %bitcast.5, s32[1,264]{1,0:T(1,128)} %bitcast.7, s32[264]{0:T(512)} %octant_ref.1), custom_call_target="tpu_custom_call" | custom-call | flops 49999998976 | bytes 1000000 | tf_op jit(solution)/shard_map/pack/pallas_call | solution.py:353
  1.6 2.0 %collective-permute-start.2 = (bf16[4,544]{1,0:T(4,128)(2,1)}, bf16[4,544]{1,0:T(4,128)(2,1)S(1)}, u32[]{:S(2)}, u32[]{:S(2)}) collective-permute-start(bf16[4,544]{1,0:T(4,128)(2,1)} %get-tuple-element.8), channel_id=1, source_target_pairs={{0,8},{8,0},{16,24},{24,16},{1,9},{9,1},{17,25},{25,17},{2,10},{10... | collective-permute-start | bytes 13064 | tf_op jit(solution)/shard_map/ppermute | solution.py:363
  3.7 1.2 %collective-permute-start.1 = (bf16[4,544]{1,0:T(4,128)(2,1)}, bf16[4,544]{1,0:T(4,128)(2,1)S(1)}, u32[]{:S(2)}, u32[]{:S(2)}) collective-permute-start(bf16[4,544]{1,0:T(4,128)(2,1)} %get-tuple-element.8), channel_id=1, source_target_pairs={{0,16},{8,24},{16,0},{24,8},{1,17},{9,25},{17,1},{25,9},{2,18},{10... | collective-permute-start | bytes 13064 | tf_op jit(solution)/shard_map/ppermute | solution.py:363
  4.9 0.0 collective-permute-start
  4.9 7.3 %all-to-all-start = ((bf16[32,4,544]{2,1,0:T(4,128)(2,1)}), bf16[32,4,544]{2,1,0:T(4,128)(2,1)S(1)}, u32[]{:S(2)}, u32[]{:S(2)}) async-start(bf16[32,4,544]{2,1,0:T(4,128)(2,1)} %get-tuple-element.7), calls=%async_computation | async-start | bytes 327680 | tf_op jit(solution)/shard_map/all_to_all | solution.py:366
  12.2 0.0 copy-start.1
  12.2 0.0 collective-permute-done.2.refs_4_
  12.2 0.0 collective-permute-done.1.refs_3_
  12.3 0.0 collective-permute-done.refs_2_
  12.3 0.0 copy-done
  12.3 0.0 copy-done.2
  12.3 0.0 copy-done.3
  12.3 24.6 %near.1.refs_2_ = f32[4,2112]{1,0:T(4,128)S(1)} custom-call(bf16[3,544]{1,0:T(4,128)(2,1)S(1)} %bitcast.6, s32[1,264]{1,0:T(1,128)S(1)} %bitcast.8, bf16[4,544]{1,0:T(4,128)(2,1)S(1)} %collective-permute-done.refs_2_, bf16[4,544]{1,0:T(4,128)(2,1)S(1)} %collective-permute-done.1.refs_3_, bf16[4,544]{1,0:T(4,128)(2,1)S(1)} %collective-permute-done.2.refs_4_, ...), custom_call_target="tpu_custom_call" | custom-call | flops 49999998976 | bytes 1000000 | tf_op jit(solution)/shard_map/near/pallas_call | solution.py:370
  36.9 0.0 all-to-all-done.refs_1_
  36.9 0.0 copy-done.1
  36.9 5.3 %far.1 = f32[3,1,544]{2,1,0:T(1,128)} custom-call(s32[1,8]{1,0:T(1,128)S(1)} %copy-done.1, bf16[32,4,544]{2,1,0:T(4,128)(2,1)S(1)} %all-to-all-done.refs_1_, f32[4,2112]{1,0:T(4,128)S(1)} %near.1.refs_2_, bf16[544,2112]{1,0:T(8,128)(2,1)S(1)} %copy-done, bf16[152,2112]{1,0:T(8,128)(2,1)} %bitcast.10, bf16[456,456]{1,0:T(8,128)(2,1)} %refs_5_.3, ...), custom_call_target="tpu_custom_call" | custom-call | tf_op jit(solution)/shard_map/far/pallas_call | solution.py:385
Async XLA Ops:
  0.0 12.3 %copy-start = (bf16[544,2112]{1,0:T(8,128)(2,1)S(1)}, bf16[544,2112]{1,0:T(8,128)(2,1)}, u32[]{:S(2)}) copy-start(bf16[544,2112]{1,0:T(8,128)(2,1)} %refs_3_.1) | copy-start | bytes 6893572
  0.0 12.3 %copy-start.2 = (bf16[1,3,544]{2,1,0:T(4,128)(2,1)S(1)}, bf16[1,3,544]{2,1,0:T(4,128)(2,1)}, u32[]{:S(2)}) copy-start(bf16[1,3,544]{2,1,0:T(4,128)(2,1)} %param.10) | copy-start | bytes 9796
  0.0 12.3 %copy-start.3 = (s32[264,1]{0,1:T(1,128)S(1)}, s32[264,1]{0,1:T(1,128)}, u32[]{:S(2)}) copy-start(s32[264,1]{0,1:T(1,128)} %param.17) | copy-start | bytes 3172
  1.6 10.6 %collective-permute-start.2 = (bf16[4,544]{1,0:T(4,128)(2,1)}, bf16[4,544]{1,0:T(4,128)(2,1)S(1)}, u32[]{:S(2)}, u32[]{:S(2)}) collective-permute-start(bf16[4,544]{1,0:T(4,128)(2,1)} %get-tuple-element.8), channel_id=1, source_target_pairs={{0,8},{8,0},{16,24},{24,16},{1,9},{9,1},{17,25},{25,17},{2,10},{10... | collective-permute-start | bytes 13064 | tf_op jit(solution)/shard_map/ppermute | solution.py:363
  3.7 8.6 %collective-permute-start.1 = (bf16[4,544]{1,0:T(4,128)(2,1)}, bf16[4,544]{1,0:T(4,128)(2,1)S(1)}, u32[]{:S(2)}, u32[]{:S(2)}) collective-permute-start(bf16[4,544]{1,0:T(4,128)(2,1)} %get-tuple-element.8), channel_id=1, source_target_pairs={{0,16},{8,24},{16,0},{24,8},{1,17},{9,25},{17,1},{25,9},{2,18},{10... | collective-permute-start | bytes 13064 | tf_op jit(solution)/shard_map/ppermute | solution.py:363
  4.9 7.3 %collective-permute-start = (bf16[4,544]{1,0:T(4,128)(2,1)}, bf16[4,544]{1,0:T(4,128)(2,1)S(1)}, u32[]{:S(2)}, u32[]{:S(2)}) collective-permute-start(bf16[4,544]{1,0:T(4,128)(2,1)} %get-tuple-element.8), channel_id=1, source_target_pairs={{0,24},{8,16},{16,8},{24,0},{1,25},{9,17},{17,9},{25,1},{2,26},{10... | collective-permute-start | bytes 13064 | tf_op jit(solution)/shard_map/ppermute | solution.py:363
  4.9 31.9 %all-to-all-start = ((bf16[32,4,544]{2,1,0:T(4,128)(2,1)}), bf16[32,4,544]{2,1,0:T(4,128)(2,1)S(1)}, u32[]{:S(2)}, u32[]{:S(2)}) async-start(bf16[32,4,544]{2,1,0:T(4,128)(2,1)} %get-tuple-element.7), calls=%async_computation | async-start | bytes 327680 | tf_op jit(solution)/shard_map/all_to_all | solution.py:366
  12.2 24.6 %copy-start.1 = (s32[1,8]{1,0:T(1,128)S(1)}, s32[1,8]{1,0:T(1,128)}, u32[]{:S(2)}) copy-start(s32[1,8]{1,0:T(1,128)} %refs_0_.1) | copy-start | bytes 100

commit v3 on v2

--- a/solution.py
+++ b/solution.py
@@ -12,6 +12,7 @@
 EXPAND_LIMIT = 128.0
 TILE = 256
 OCTANTS_PER_OWNER = 2
+COPY_TILES = 3
 F32 = jnp.float32
 BF16 = jnp.bfloat16
 LANES = (((1,), (1,)), ((), ()))
@@ -34,36 +35,17 @@
     return high, (x - high.astype(F32)).astype(BF16)
 
 
-def row_chunks(rows):
-    return [(start, min(start + TILE, rows)) for start in range(0, rows, TILE)]
-
-
-class Arriving:
-    def __init__(self, sources, targets, sems):
-        self.targets = targets
-        self.pieces = [
-            [
-                (pltpu.make_async_copy(src.at[a:b], dst.at[a:b], sems.at[n, i]), a, b)
-                for i, (a, b) in enumerate(row_chunks(src.shape[0]))
-            ]
-            for n, (src, dst) in enumerate(zip(sources, targets))
-        ]
-
-    def start(self, n):
-        for copy, _, _ in self.pieces[n]:
-            copy.start()
-
-    def wait(self, n):
-        for copy, _, _ in self.pieces[n]:
-            copy.wait()
-
-    def dot(self, lhs, n):
-        total = None
-        for copy, a, b in self.pieces[n]:
-            copy.wait()
-            part = dot(lhs[:, a:b], self.targets[n][a:b, :])
-            total = part if total is None else total + part
-        return total
+def lane_chunks(lanes, tiles):
+    return [(start, min(start + tiles * TILE, lanes)) for start in range(0, lanes, tiles * TILE)]
+
+
+def in_stages(*stages):
+    def step(at, _):
+        for n, stage in enumerate(stages):
+            pl.when(at == n)(stage)
+        return 0
+
+    lax.fori_loop(0, len(stages), step, 0)
 
 
 def pack_kernel(cell_ref, owner_ref, octant_ref, pack_ref, spread_ref):
@@ -176,44 +158,73 @@
 
 def near_kernel(blk, packs_given, *refs):
     cell_ref, owner_ref, *pack_refs = refs[: packs_given + 2]
-    bend_ref, up_hbm, out_ref, up_ref, rows_ref, found_ref, sems = refs[packs_given + 2 :]
-    arriving = Arriving([up_hbm], [up_ref], sems)
-    arriving.start(0)
-    packs = [ref[...].astype(F32) for ref in pack_refs]
-    cells = len(packs) + 1
+    bend_ref, up_hbm, out_ref, up_ref, *refs = refs[packs_given + 2 :]
+    places_ref, bent_ref, sort_ref, part_ref, rows_ref, found_ref, sems = refs
+    chunks = lane_chunks(up_ref.shape[1], COPY_TILES)
+    copies = [
+        pltpu.make_async_copy(up_hbm.at[:, a:b], up_ref.at[:, a:b], sems.at[n])
+        for n, (a, b) in enumerate(chunks)
+    ]
+    for copy in copies:
+        copy.start()
+    cells = packs_given + 1
     fine = up_ref.shape[1]
     nb = fine // blk
     capacity = nb // cells + 2
     spots = cells * capacity
     group = TILE // blk
     tiles = -(-fine // TILE)
-    point_rows, force_rows = [], []
-    coarse = [jnp.concatenate([cell_ref[...].astype(F32), jnp.zeros((1, cell_ref.shape[1]), F32)], axis=0)]
-    coarse += [jnp.where(iota(pack.shape, 0) < 3, pack, 0.0) for pack in packs]
-    owners = [owner_ref[...].astype(F32)] + [pack[3:4, 0:nb] for pack in packs]
-    for three in coarse:
-        point_rows += [three, jnp.zeros_like(three)]
-        force_rows += [jnp.zeros_like(three), three]
-    point_rows = jnp.concatenate(point_rows, axis=0).astype(BF16)
-    force_rows = jnp.concatenate(force_rows, axis=0).astype(BF16)
-    leaf_ids = iota((cells, nb), 0).astype(F32)
-    chosen = jnp.concatenate([(leaf_ids == own).astype(F32) for own in owners], axis=0)
-    earlier = (iota((nb, nb), 0) < iota((nb, nb), 1)).astype(BF16)
-    before = dot(chosen.astype(BF16), earlier) * chosen
-    spot_ids = iota((spots, nb), 0).astype(F32)
-    sorts = []
-    for c in range(cells):
-        rank = jnp.sum(before[c * cells : (c + 1) * cells], axis=0, keepdims=True)
-        sorts.append((spot_ids == owners[c] * capacity + rank).astype(BF16))
+
+    def prepare():
+        packs = [ref[...].astype(F32) for ref in pack_refs]
+        none = jnp.zeros((1, cell_ref.shape[1]), F32)
+        coarse = [jnp.concatenate([cell_ref[...].astype(F32), none], axis=0)]
+        coarse += [jnp.where(iota(pack.shape, 0) < 3, pack, 0.0) for pack in packs]
+        owners = [owner_ref[...].astype(F32)] + [pack[3:4, 0:nb] for pack in packs]
+        point_rows, force_rows = [], []
+        for three in coarse:
+            point_rows += [three, jnp.zeros_like(three)]
+            force_rows += [jnp.zeros_like(three), three]
+        places_ref[...] = jnp.concatenate(point_rows, axis=0).astype(BF16)
+        force_rows = jnp.concatenate(force_rows, axis=0).astype(BF16)
+        bent_ref[...] = dot(force_rows, bend_ref[...])
+        leaf_ids = iota((cells, nb), 0).astype(F32)
+        chosen = jnp.concatenate([(leaf_ids == own).astype(F32) for own in owners], axis=0)
+        earlier = (iota((nb, nb), 0) < iota((nb, nb), 1)).astype(BF16)
+        before = dot(chosen.astype(BF16), earlier) * chosen
+        spot_ids = iota((spots, nb), 0).astype(F32)
+        for c in range(cells):
+            rank = jnp.sum(before[c * cells : (c + 1) * cells], axis=0, keepdims=True)
+            sort_ref[c] = (spot_ids == owners[c] * capacity + rank).astype(BF16)
+
+    def part_points(n):
+        a, b = chunks[n]
+        copies[n].wait()
+        fields = (bent_ref[:, a:b] + dot(places_ref[...], up_ref[:, a:b])).astype(BF16)
+        if (b - a) % TILE:
+            rest = jnp.zeros((8 * cells, -(b - a) % TILE), BF16)
+            fields = jnp.concatenate([fields, rest], axis=1)
+        stacked = [fields[:, t : t + TILE] for t in range(0, fields.shape[1], TILE)]
+        parted = dot(jnp.concatenate(stacked, axis=0), interleave_matrix(blk))
+        first = a // TILE * 8 * cells
+        part_ref[first : first + parted.shape[0]] = parted
+
+    def finish():
+        near_sums(blk, cells, fine, out_ref, sort_ref, part_ref, rows_ref, found_ref)
+
+    in_stages(
+        prepare, *[functools.partial(part_points, n) for n in range(len(chunks))], finish
+    )
+
+
+def near_sums(blk, cells, fine, out_ref, sort_ref, part_ref, rows_ref, found_ref):
+    nb = fine // blk
+    capacity = nb // cells + 2
+    group = TILE // blk
+    tiles = -(-fine // TILE)
     mix = interleave_matrix(blk)
-    fields = (dot(force_rows, bend_ref[...]) + arriving.dot(point_rows, 0)).astype(BF16)
-    fields = jnp.concatenate(
-        [fields, jnp.zeros((8 * cells, tiles * TILE - fine), BF16)], axis=1
-    )
-    stacked = jnp.concatenate(
-        [fields[:, t * TILE : (t + 1) * TILE] for t in range(tiles)], axis=0
-    )
-    parted = dot(stacked, mix)
+    parted = part_ref[...]
+    sorts = [sort_ref[c] for c in range(cells)]
     by_point = [
         jnp.concatenate(
             [
@@ -273,12 +284,14 @@
         out_ref[0:4, t * TILE : stop] = natural[4 * t : 4 * t + 4, 0 : stop - t * TILE]
 
 def far_kernel(blk, cells, regions, *refs):
-    list_ref, packs_ref, near_ref, bend_ref, *in_hbm = refs[:8]
-    out_ref, *in_vmem, sems = refs[8:]
-    dens_ref, trans_ref, eval_ref, smooth_ref = in_vmem
-    arriving = Arriving(in_hbm, in_vmem, sems)
-    for n in range(len(in_hbm)):
-        arriving.start(n)
+    list_ref, packs_ref, near_ref, bend_ref, dens_ref, *in_hbm = refs[:8]
+    out_ref, trans_ref, eval_ref, smooth_ref, density_ref, total_ref, sems = refs[8:]
+    trans_copy, eval_copy, smooth_copy = [
+        pltpu.make_async_copy(src, dst, sems.at[n])
+        for n, (src, dst) in enumerate(zip(in_hbm, (trans_ref, eval_ref, smooth_ref)))
+    ]
+    for copy in (trans_copy, eval_copy, smooth_copy):
+        copy.start()
     listed = list_ref.shape[1]
     fine = bend_ref.shape[1]
     nb = fine // blk
@@ -286,43 +299,52 @@
     per_region = OCTANTS_PER_OWNER * cells
     rows = cells * 3 * listed
     devices = cells * regions
-    row = iota((rows, 1), 0)
-    entry, comp, cell = row % listed, row // listed % 3, row // (3 * listed)
-    octant = jnp.zeros((rows, 1), jnp.int32)
-    region = jnp.zeros((rows, 1), jnp.int32)
-    for l in range(listed):
-        wanted = list_ref[0, l]
-        octant = jnp.where(entry == l, wanted % per_region, octant)
-        region = jnp.where(entry == l, wanted // per_region, region)
-    source = (cell * regions + region) * 4
-    columns = iota((rows, devices * 4), 1)
-    flat = packs_ref[...].reshape(devices * 4, packs_ref.shape[2])
-    coarse = dot((columns == source + comp).astype(BF16), flat)
-    marks = dot((columns == source + 3).astype(BF16), flat)
-    inside = (marks[:, nb : 2 * nb] == octant.astype(F32)).astype(BF16)
-    widen = (iota((nb, fine), 0) == iota((nb, fine), 1) // blk).astype(BF16)
-    inside = dot(inside, widen)
-    forces = dot(coarse.astype(BF16), bend_ref[...]).astype(BF16).astype(F32)
-    arriving.wait(0)
-    density = dot_lanes((forces * inside).astype(BF16), dens_ref[...])
     span = 3 * listed
-    density = sum(density[c * span : (c + 1) * span] for c in range(cells)).astype(BF16)
-    arriving.wait(1)
-    expansion = sum(
-        dot(density[k * listed : (k + 1) * listed], trans_ref[k * points : (k + 1) * points, :])
-        for k in range(3)
-    )
-    far = jnp.sum(expansion.astype(BF16).astype(F32), axis=0, keepdims=True)
-    far = jnp.concatenate(
-        [far[:, k * points : (k + 1) * points] for k in range(3)] + [jnp.zeros((1, points), F32)],
-        axis=0,
-    )
-    arriving.wait(2)
-    total = near_ref[0:4, :] + dot(far.astype(BF16), eval_ref[...])
-    arriving.wait(3)
-    velocity = dot_lanes(total.astype(BF16), smooth_ref[...])
-    for k in range(3):
-        out_ref[k] = velocity[k : k + 1]
+
+    def densities():
+        row = iota((rows, 1), 0)
+        entry, comp, cell = row % listed, row // listed % 3, row // span
+        octant = jnp.zeros((rows, 1), jnp.int32)
+        region = jnp.zeros((rows, 1), jnp.int32)
+        for l in range(listed):
+            wanted = list_ref[0, l]
+            octant = jnp.where(entry == l, wanted % per_region, octant)
+            region = jnp.where(entry == l, wanted // per_region, region)
+        source = (cell * regions + region) * 4
+        columns = iota((rows, devices * 4), 1)
+        flat = packs_ref[...].reshape(devices * 4, packs_ref.shape[2])
+        coarse = dot((columns == source + comp).astype(BF16), flat)
+        marks = dot((columns == source + 3).astype(BF16), flat)
+        inside = (marks[:, nb : 2 * nb] == octant.astype(F32)).astype(BF16)
+        widen = (iota((nb, fine), 0) == iota((nb, fine), 1) // blk).astype(BF16)
+        inside = dot(inside, widen)
+        forces = dot(coarse.astype(BF16), bend_ref[...]).astype(BF16).astype(F32)
+        density = dot_lanes((forces * inside).astype(BF16), dens_ref[...])
+        density_ref[...] = sum(density[c * span : (c + 1) * span] for c in range(cells))
+
+    def totals():
+        trans_copy.wait()
+        eval_copy.wait()
+        density = density_ref[...].astype(BF16)
+        expansion = sum(
+            dot(density[k * listed : (k + 1) * listed], trans_ref[k * points : (k + 1) * points, :])
+            for k in range(3)
+        )
+        far = jnp.sum(expansion.astype(BF16).astype(F32), axis=0, keepdims=True)
+        far = jnp.concatenate(
+            [far[:, k * points : (k + 1) * points] for k in range(3)]
+            + [jnp.zeros((1, points), F32)],
+            axis=0,
+        )
+        total_ref[...] = near_ref[0:4, :] + dot(far.astype(BF16), eval_ref[...])
+
+    def velocities():
+        smooth_copy.wait()
+        velocity = dot_lanes(total_ref[...].astype(BF16), smooth_ref[...])
+        for k in range(3):
+            out_ref[k] = velocity[k : k + 1]
+
+    in_stages(densities, totals, velocities)
 
 
 def in_place(x):
@@ -373,24 +395,32 @@
         in_specs=[in_vmem] * (cells + 2) + [in_hbm],
         scratch_shapes=[
             pltpu.VMEM(upsample.shape, BF16),
+            pltpu.VMEM((8 * cells, coarse), BF16),
+            pltpu.VMEM((8 * cells, fine), F32),
+            pltpu.VMEM((cells, points // blk, nb), BF16),
+            pltpu.VMEM((-(-fine // TILE) * 8 * cells, TILE), F32),
             pltpu.VMEM((cells, 8, points), F32),
             pltpu.VMEM((cells, 4 * blk, points // (cells * blk)), F32),
-            pltpu.SemaphoreType.DMA((1, len(row_chunks(coarse)))),
+            pltpu.SemaphoreType.DMA((len(lane_chunks(fine, COPY_TILES)),)),
         ],
         compiler_params=vmem(40),
         cost_estimate=pl.CostEstimate(flops=5 * 10**10, bytes_accessed=10**6, transcendentals=0),
         name="near",
     )(own_cell, own_blocks, *others, bending, in_place(upsample))
-    later = [in_place(x) for x in (to_density.T, translate, evaluate, smoothing.T)]
+    later = [in_place(x) for x in (translate, evaluate, smoothing.T)]
     velocity = pl.pallas_call(
         functools.partial(far_kernel, blk, cells, regions),
         out_shape=jax.ShapeDtypeStruct((3, 1, coarse), F32),
-        in_specs=[pl.BlockSpec(memory_space=pltpu.SMEM)] + [in_vmem] * 3 + [in_hbm] * 4,
+        in_specs=[pl.BlockSpec(memory_space=pltpu.SMEM)] + [in_vmem] * 4 + [in_hbm] * 3,
         scratch_shapes=[pltpu.VMEM(x.shape, BF16) for x in later]
-        + [pltpu.SemaphoreType.DMA((4, len(row_chunks(coarse))))],
+        + [
+            pltpu.VMEM((3 * far_list.shape[1], evaluate.shape[0]), F32),
+            pltpu.VMEM((4, fine), F32),
+            pltpu.SemaphoreType.DMA((3,)),
+        ],
         compiler_params=vmem(32),
         name="far",
-    )(far_list, everyone, near, bending, *later)
+    )(far_list, everyone, near, bending, to_density.T, *later)
     return velocity.transpose(1, 0, 2)
 
 

time: 42.5 us -> 40.1 us (0.944)
  the two profiles are of different devices: /device:TPU:1 before, /device:TPU:9 now
where the time goes in v3:
time: 40.1 us; the launch traced here: 39.5 us
  Pallas kernels  29.5 us (74%)
  starting transfers between devices  9.85 us (25%)
    pallas_call x1, Pallas kernels, on_device(): pl.pallas_call(functools.partial(near_kernel, blk, len(others)), out_shap...  24 us
    all_to_all x1, starting transfers between devices, on_device(): lax.all_to_all(spread, ('cells', 'region'), split_axis=0, concat_axis=0,...  7.2 us
    pallas_call x1, Pallas kernels, on_device(): pl.pallas_call(functools.partial(far_kernel, blk, cells, regions), out_sh...  3.92 us
    ppermute x3, starting transfers between devices, on_device(): lax.ppermute(pack, 'cells', [(i, i ^ k) for i in range(cells)])  2.65 us
    pallas_call x1, Pallas kernels, on_device(): pl.pallas_call(pack_kernel, out_shape=(jax.ShapeDtypeStruct((4, coarse),...  1.62 us
  transfers between devices with their start and end apart: 4, of which 0 were waited for; matrix products, arithmetic and copies ran while one was open for 0% of the time, Pallas kernels for 61%

profile of v3, /device:TPU:9, one launch (start us, length us, event | category | flops | bytes accessed | tf_op | source)
XLA Modules:
  0.0 39.5 jit_solution(11353254662845950623)
XLA Ops:
  0.0 0.0 copy-start
  0.0 0.0 copy-start.3
  0.0 0.0 copy-start.4
  0.0 1.6 %pack.1 = (bf16[4,544]{1,0:T(4,128)(2,1)}, bf16[32,4,544]{2,1,0:T(4,128)(2,1)}) custom-call(bf16[3,544]{1,0:T(4,128)(2,1)} %bitcast.6, s32[1,264]{1,0:T(1,128)} %bitcast.8, s32[264]{0:T(512)} %octant_ref.1), custom_call_target="tpu_custom_call" | custom-call | flops 49999998976 | bytes 1000000 | tf_op jit(solution)/shard_map/pack/pallas_call | solution.py:375
  1.6 1.2 %collective-permute-start.2 = (bf16[4,544]{1,0:T(4,128)(2,1)}, bf16[4,544]{1,0:T(4,128)(2,1)S(1)}, u32[]{:S(2)}, u32[]{:S(2)}) collective-permute-start(bf16[4,544]{1,0:T(4,128)(2,1)} %get-tuple-element.8), channel_id=1, source_target_pairs={{0,8},{8,0},{16,24},{24,16},{1,9},{9,1},{17,25},{25,17},{2,10},{10... | collective-permute-start | bytes 13064 | tf_op jit(solution)/shard_map/ppermute | solution.py:385
  2.8 1.2 %collective-permute-start.1 = (bf16[4,544]{1,0:T(4,128)(2,1)}, bf16[4,544]{1,0:T(4,128)(2,1)S(1)}, u32[]{:S(2)}, u32[]{:S(2)}) collective-permute-start(bf16[4,544]{1,0:T(4,128)(2,1)} %get-tuple-element.8), channel_id=1, source_target_pairs={{0,16},{8,24},{16,0},{24,8},{1,17},{9,25},{17,1},{25,9},{2,18},{10... | collective-permute-start | bytes 13064 | tf_op jit(solution)/shard_map/ppermute | solution.py:385
  4.1 0.2 collective-permute-start
  4.3 7.2 %all-to-all-start = ((bf16[32,4,544]{2,1,0:T(4,128)(2,1)}), bf16[32,4,544]{2,1,0:T(4,128)(2,1)S(1)}, u32[]{:S(2)}, u32[]{:S(2)}) async-start(bf16[32,4,544]{2,1,0:T(4,128)(2,1)} %get-tuple-element.7), calls=%async_computation | async-start | bytes 327680 | tf_op jit(solution)/shard_map/all_to_all | solution.py:388
  11.5 0.0 copy-start.1
  11.5 0.0 copy-start.2
  11.5 0.0 collective-permute-done.2.refs_4_
  11.5 0.0 collective-permute-done.1.refs_3_
  11.5 0.0 collective-permute-done.refs_2_
  11.5 0.0 copy-done
  11.6 0.0 copy-done.3
  11.6 0.0 copy-done.4
  11.6 24.0 %near.1.refs_2_ = f32[4,2112]{1,0:T(4,128)S(1)} custom-call(bf16[3,544]{1,0:T(4,128)(2,1)S(1)} %bitcast.7, s32[1,264]{1,0:T(1,128)S(1)} %bitcast.9, bf16[4,544]{1,0:T(4,128)(2,1)S(1)} %collective-permute-done.refs_2_, bf16[4,544]{1,0:T(4,128)(2,1)S(1)} %collective-permute-done.1.refs_3_, bf16[4,544]{1,0:T(4,128)(2,1)S(1)} %collective-permute-done.2.refs_4_, ...), custom_call_target="tpu_custom_call" | custom-call | flops 49999998976 | bytes 1000000 | tf_op jit(solution)/shard_map/near/pallas_call | solution.py:392
  35.6 0.0 all-to-all-done.refs_1_
  35.6 0.0 copy-done.1
  35.6 0.0 copy-done.2
  35.6 3.9 %far.1 = f32[3,1,544]{2,1,0:T(1,128)} custom-call(s32[1,8]{1,0:T(1,128)S(1)} %copy-done.2, bf16[32,4,544]{2,1,0:T(4,128)(2,1)S(1)} %all-to-all-done.refs_1_, f32[4,2112]{1,0:T(4,128)S(1)} %near.1.refs_2_, bf16[544,2112]{1,0:T(8,128)(2,1)S(1)} %copy-done, bf16[152,2112]{1,0:T(8,128)(2,1)S(1)} %bitcast.5, bf16[456,456]{1,0:T(8,128)(2,1)} %refs_5_.3, ...), custom_call_target="tpu_custom_call" | custom-call | tf_op jit(solution)/shard_map/far/pallas_call | solution.py:411
Async XLA Ops:
  0.0 11.5 %copy-start = (bf16[544,2112]{1,0:T(8,128)(2,1)S(1)}, bf16[544,2112]{1,0:T(8,128)(2,1)}, u32[]{:S(2)}) copy-start(bf16[544,2112]{1,0:T(8,128)(2,1)} %refs_3_.1) | copy-start | bytes 6893572
  0.0 11.6 %copy-start.3 = (bf16[1,3,544]{2,1,0:T(4,128)(2,1)S(1)}, bf16[1,3,544]{2,1,0:T(4,128)(2,1)}, u32[]{:S(2)}) copy-start(bf16[1,3,544]{2,1,0:T(4,128)(2,1)} %param.10) | copy-start | bytes 9796
  0.0 11.6 %copy-start.4 = (s32[264,1]{0,1:T(1,128)S(1)}, s32[264,1]{0,1:T(1,128)}, u32[]{:S(2)}) copy-start(s32[264,1]{0,1:T(1,128)} %param.17) | copy-start | bytes 3172
  1.6 9.9 %collective-permute-start.2 = (bf16[4,544]{1,0:T(4,128)(2,1)}, bf16[4,544]{1,0:T(4,128)(2,1)S(1)}, u32[]{:S(2)}, u32[]{:S(2)}) collective-permute-start(bf16[4,544]{1,0:T(4,128)(2,1)} %get-tuple-element.8), channel_id=1, source_target_pairs={{0,8},{8,0},{16,24},{24,16},{1,9},{9,1},{17,25},{25,17},{2,10},{10... | collective-permute-start | bytes 13064 | tf_op jit(solution)/shard_map/ppermute | solution.py:385
  2.8 8.7 %collective-permute-start.1 = (bf16[4,544]{1,0:T(4,128)(2,1)}, bf16[4,544]{1,0:T(4,128)(2,1)S(1)}, u32[]{:S(2)}, u32[]{:S(2)}) collective-permute-start(bf16[4,544]{1,0:T(4,128)(2,1)} %get-tuple-element.8), channel_id=1, source_target_pairs={{0,16},{8,24},{16,0},{24,8},{1,17},{9,25},{17,1},{25,9},{2,18},{10... | collective-permute-start | bytes 13064 | tf_op jit(solution)/shard_map/ppermute | solution.py:385
  4.1 7.5 %collective-permute-start = (bf16[4,544]{1,0:T(4,128)(2,1)}, bf16[4,544]{1,0:T(4,128)(2,1)S(1)}, u32[]{:S(2)}, u32[]{:S(2)}) collective-permute-start(bf16[4,544]{1,0:T(4,128)(2,1)} %get-tuple-element.8), channel_id=1, source_target_pairs={{0,24},{8,16},{16,8},{24,0},{1,25},{9,17},{17,9},{25,1},{2,26},{10... | collective-permute-start | bytes 13064 | tf_op jit(solution)/shard_map/ppermute | solution.py:385
  4.3 31.3 %all-to-all-start = ((bf16[32,4,544]{2,1,0:T(4,128)(2,1)}), bf16[32,4,544]{2,1,0:T(4,128)(2,1)S(1)}, u32[]{:S(2)}, u32[]{:S(2)}) async-start(bf16[32,4,544]{2,1,0:T(4,128)(2,1)} %get-tuple-element.7), calls=%async_computation | async-start | bytes 327680 | tf_op jit(solution)/shard_map/all_to_all | solution.py:388
  11.5 24.1 %copy-start.1 = (bf16[2112,152]{0,1:T(8,128)(2,1)S(1)}, bf16[2112,152]{0,1:T(8,128)(2,1)}, u32[]{:S(2)}) copy-start(bf16[2112,152]{0,1:T(8,128)(2,1)} %param.13) | copy-start | bytes 1926148
  11.5 24.1 %copy-start.2 = (s32[1,8]{1,0:T(1,128)S(1)}, s32[1,8]{1,0:T(1,128)}, u32[]{:S(2)}) copy-start(s32[1,8]{1,0:T(1,128)} %refs_0_.1) | copy-start | bytes 100

commit v4 on v3

--- a/solution.py
+++ b/solution.py
@@ -13,6 +13,7 @@
 TILE = 256
 OCTANTS_PER_OWNER = 2
 COPY_TILES = 3
+SOURCE_TILES = 5
 F32 = jnp.float32
 BF16 = jnp.bfloat16
 LANES = (((1,), (1,)), ((), ()))
@@ -48,21 +49,28 @@
     lax.fori_loop(0, len(stages), step, 0)
 
 
+def spread_rows(coarse, nb):
+    whole, rest = coarse // TILE, coarse % TILE
+    return whole, rest, 3 * whole + -(-(3 * rest + nb) // TILE)
+
+
 def pack_kernel(cell_ref, owner_ref, octant_ref, pack_ref, spread_ref):
     nb = owner_ref.shape[1]
-    width = cell_ref.shape[1]
-    octant = octant_ref[...].reshape(1, nb)
-    pack_ref[0:3, :] = cell_ref[...]
-    row = jnp.concatenate(
-        [
-            owner_ref[...].astype(F32),
-            octant.astype(F32),
-            jnp.zeros((1, width - 2 * nb), F32),
-        ],
-        axis=1,
+    coarse = cell_ref.shape[1]
+    whole, rest, height = spread_rows(coarse, nb)
+    cell = cell_ref[...].astype(F32)
+    owner = jnp.concatenate(
+        [owner_ref[...].astype(F32), jnp.zeros((1, coarse - nb), F32)], axis=1
     )
-    pack_ref[3:4, :] = row.astype(BF16)
-    spread_ref[...] = jnp.broadcast_to(pack_ref[...][None], spread_ref.shape)
+    pack_ref[...] = jnp.concatenate([cell, owner], axis=0).astype(BF16)
+    rows = [cell[k : k + 1, t * TILE : (t + 1) * TILE] for k in range(3) for t in range(whole)]
+    tail = [cell[k : k + 1, whole * TILE :] for k in range(3)]
+    tail.append(octant_ref[...].reshape(1, nb).astype(F32))
+    tail.append(jnp.zeros((1, (height - 3 * whole) * TILE - 3 * rest - nb), F32))
+    tail = jnp.concatenate(tail, axis=1)
+    rows += [tail[:, t : t + TILE] for t in range(0, tail.shape[1], TILE)]
+    rows = jnp.concatenate(rows, axis=0).astype(BF16)
+    spread_ref[...] = jnp.broadcast_to(rows[None], spread_ref.shape)
 
 
 def interleave_matrix(blk):
@@ -116,9 +124,13 @@
 def expanded_sums(rows, targets):
     columns = source_columns(rows)
     source, target = distance_factors(rows, targets)
-    inverse = lax.rsqrt(dot(target, source))
-    cubed = (inverse * inverse * inverse).astype(BF16)
-    sums = dot_lanes(columns, cubed)
+    sums = None
+    for start in range(0, rows.shape[1], SOURCE_TILES * TILE):
+        part = slice(start, min(start + SOURCE_TILES * TILE, rows.shape[1]))
+        inverse = lax.rsqrt(dot(target, source[:, part]))
+        cubed = (inverse * inverse * inverse).astype(BF16)
+        some = dot_lanes(columns[:, part], cubed)
+        sums = some if sums is None else sums + some
     place = targets[0:4]
     moment = [sums[8 * k : 8 * k + 4] + sums[8 * k + 4 : 8 * k + 8] for k in range(3)]
     rest = sums[24:28] + sums[28:32] + sums[32:36]
@@ -300,6 +312,7 @@
     rows = cells * 3 * listed
     devices = cells * regions
     span = 3 * listed
+    whole, rest, height = spread_rows(bend_ref.shape[0], nb)
 
     def densities():
         row = iota((rows, 1), 0)
@@ -307,15 +320,23 @@
         octant = jnp.zeros((rows, 1), jnp.int32)
         region = jnp.zeros((rows, 1), jnp.int32)
         for l in range(listed):
-            wanted = list_ref[0, l]
+            wanted = list_ref[0:1, l : l + 1]
             octant = jnp.where(entry == l, wanted % per_region, octant)
             region = jnp.where(entry == l, wanted // per_region, region)
-        source = (cell * regions + region) * 4
-        columns = iota((rows, devices * 4), 1)
-        flat = packs_ref[...].reshape(devices * 4, packs_ref.shape[2])
-        coarse = dot((columns == source + comp).astype(BF16), flat)
-        marks = dot((columns == source + 3).astype(BF16), flat)
-        inside = (marks[:, nb : 2 * nb] == octant.astype(F32)).astype(BF16)
+        source = (cell * regions + region) * height
+        columns = iota((rows, devices * height), 1)
+        flat = packs_ref[...].reshape(devices * height, TILE)
+
+        def take(n):
+            return dot((columns == source + n).astype(BF16), flat)
+
+        coarse = [take(comp * whole + t) for t in range(whole)]
+        tail = jnp.concatenate([take(n) for n in range(3 * whole, height)], axis=1)
+        left = [tail[:, k * rest : (k + 1) * rest] for k in range(3)]
+        coarse.append(jnp.where(comp == 0, left[0], jnp.where(comp == 1, left[1], left[2])))
+        coarse = jnp.concatenate(coarse, axis=1)
+        marks = tail[:, 3 * rest : 3 * rest + nb]
+        inside = (marks == octant.astype(F32)).astype(BF16)
         widen = (iota((nb, fine), 0) == iota((nb, fine), 1) // blk).astype(BF16)
         inside = dot(inside, widen)
         forces = dot(coarse.astype(BF16), bend_ref[...]).astype(BF16).astype(F32)
@@ -376,7 +397,7 @@
         pack_kernel,
         out_shape=(
             jax.ShapeDtypeStruct((4, coarse), BF16),
-            jax.ShapeDtypeStruct((cells * regions, 4, coarse), BF16),
+            jax.ShapeDtypeStruct((cells * regions, spread_rows(coarse, nb)[2], TILE), BF16),
         ),
         cost_estimate=pl.CostEstimate(flops=5 * 10**10, bytes_accessed=10**6, transcendentals=0),
         name="pack",
@@ -411,7 +432,7 @@
     velocity = pl.pallas_call(
         functools.partial(far_kernel, blk, cells, regions),
         out_shape=jax.ShapeDtypeStruct((3, 1, coarse), F32),
-        in_specs=[pl.BlockSpec(memory_space=pltpu.SMEM)] + [in_vmem] * 4 + [in_hbm] * 3,
+        in_specs=[in_vmem] * 5 + [in_hbm] * 3,
         scratch_shapes=[pltpu.VMEM(x.shape, BF16) for x in later]
         + [
             pltpu.VMEM((3 * far_list.shape[1], evaluate.shape[0]), F32),

time: 40.1 us -> 40.5 us (level)
  the two profiles are of different devices: /device:TPU:9 before, /device:TPU:0 now
where the time goes in v4:
time: 40.5 us; the launch traced here: 40.2 us
  Pallas kernels  29.3 us (72%)
  starting transfers between devices  10.8 us (27%)
    pallas_call x1, Pallas kernels, on_device(): pl.pallas_call(functools.partial(near_kernel, blk, len(others)), out_shap...  23.9 us
    all_to_all x1, starting transfers between devices, on_device(): lax.all_to_all(spread, ('cells', 'region'), split_axis=0, concat_axis=0,...  6.32 us
    ppermute x3, starting transfers between devices, on_device(): lax.ppermute(pack, 'cells', [(i, i ^ k) for i in range(cells)])  4.46 us
    pallas_call x1, Pallas kernels, on_device(): pl.pallas_call(functools.partial(far_kernel, blk, cells, regions), out_sh...  3.78 us
    pallas_call x1, Pallas kernels, on_device(): pl.pallas_call(pack_kernel, out_shape=(jax.ShapeDtypeStruct((4, coarse),...  1.59 us
  transfers between devices with their start and end apart: 4, of which 0 were waited for; matrix products, arithmetic and copies ran while one was open for 0% of the time, Pallas kernels for 59%

profile of v4, /device:TPU:0, one launch (start us, length us, event | category | flops | bytes accessed | tf_op | source)
XLA Modules:
  0.0 40.2 jit_solution(11070437648186425112)
XLA Ops:
  0.0 0.0 copy-start
  0.0 0.0 copy-start.3
  0.0 0.0 copy-start.4
  0.0 1.6 %pack.1 = (bf16[4,544]{1,0:T(4,128)(2,1)}, bf16[32,8,256]{2,1,0:T(8,128)(2,1)}) custom-call(bf16[3,544]{1,0:T(4,128)(2,1)} %bitcast.6, s32[1,264]{1,0:T(1,128)} %bitcast.8, s32[264]{0:T(512)} %octant_ref.1), custom_call_target="tpu_custom_call" | custom-call | flops 49999998976 | bytes 1000000 | tf_op jit(solution)/shard_map/pack/pallas_call | solution.py:396
  1.6 2.9 %collective-permute-start.2 = (bf16[4,544]{1,0:T(4,128)(2,1)}, bf16[4,544]{1,0:T(4,128)(2,1)S(1)}, u32[]{:S(2)}, u32[]{:S(2)}) collective-permute-start(bf16[4,544]{1,0:T(4,128)(2,1)} %get-tuple-element.8), channel_id=1, source_target_pairs={{0,8},{8,0},{16,24},{24,16},{1,9},{9,1},{17,25},{25,17},{2,10},{10... | collective-permute-start | bytes 13064 | tf_op jit(solution)/shard_map/ppermute | solution.py:406
  4.5 1.5 %collective-permute-start.1 = (bf16[4,544]{1,0:T(4,128)(2,1)}, bf16[4,544]{1,0:T(4,128)(2,1)S(1)}, u32[]{:S(2)}, u32[]{:S(2)}) collective-permute-start(bf16[4,544]{1,0:T(4,128)(2,1)} %get-tuple-element.8), channel_id=1, source_target_pairs={{0,16},{8,24},{16,0},{24,8},{1,17},{9,25},{17,1},{25,9},{2,18},{10... | collective-permute-start | bytes 13064 | tf_op jit(solution)/shard_map/ppermute | solution.py:406
  6.1 0.0 collective-permute-start
  6.1 6.3 %all-to-all-start = ((bf16[32,8,256]{2,1,0:T(8,128)(2,1)}), bf16[32,8,256]{2,1,0:T(8,128)(2,1)S(1)}, u32[]{:S(2)}, u32[]{:S(2)}) async-start(bf16[32,8,256]{2,1,0:T(8,128)(2,1)} %get-tuple-element.7), calls=%async_computation | async-start | bytes 262144 | tf_op jit(solution)/shard_map/all_to_all | solution.py:409
  12.4 0.0 copy-start.1
  12.4 0.0 copy-start.2
  12.4 0.0 collective-permute-done.2.refs_4_
  12.4 0.0 collective-permute-done.1.refs_3_
  12.4 0.0 collective-permute-done.refs_2_
  12.5 0.0 copy-done
  12.5 0.0 copy-done.3
  12.5 0.0 copy-done.4
  12.5 23.9 %near.1.refs_2_ = f32[4,2112]{1,0:T(4,128)S(1)} custom-call(bf16[3,544]{1,0:T(4,128)(2,1)S(1)} %bitcast.7, s32[1,264]{1,0:T(1,128)S(1)} %bitcast.9, bf16[4,544]{1,0:T(4,128)(2,1)S(1)} %collective-permute-done.refs_2_, bf16[4,544]{1,0:T(4,128)(2,1)S(1)} %collective-permute-done.1.refs_3_, bf16[4,544]{1,0:T(4,128)(2,1)S(1)} %collective-permute-done.2.refs_4_, ...), custom_call_target="tpu_custom_call" | custom-call | flops 49999998976 | bytes 1000000 | tf_op jit(solution)/shard_map/near/pallas_call | solution.py:413
  36.4 0.0 all-to-all-done.refs_1_
  36.4 0.0 copy-done.1
  36.4 0.0 copy-done.2
  36.4 3.8 %far.1 = f32[3,1,544]{2,1,0:T(1,128)} custom-call(s32[1,8]{1,0:T(1,128)S(1)} %copy-done.2, bf16[32,8,256]{2,1,0:T(8,128)(2,1)S(1)} %all-to-all-done.refs_1_, f32[4,2112]{1,0:T(4,128)S(1)} %near.1.refs_2_, bf16[544,2112]{1,0:T(8,128)(2,1)S(1)} %copy-done, bf16[152,2112]{1,0:T(8,128)(2,1)S(1)} %bitcast.5, bf16[456,456]{1,0:T(8,128)(2,1)} %refs_5_.3, ...), custom_call_target="tpu_custom_call" | custom-call | tf_op jit(solution)/shard_map/far/pallas_call | solution.py:432
Async XLA Ops:
  0.0 12.5 %copy-start = (bf16[544,2112]{1,0:T(8,128)(2,1)S(1)}, bf16[544,2112]{1,0:T(8,128)(2,1)}, u32[]{:S(2)}) copy-start(bf16[544,2112]{1,0:T(8,128)(2,1)} %refs_3_.1) | copy-start | bytes 6893572
  0.0 12.5 %copy-start.3 = (bf16[1,3,544]{2,1,0:T(4,128)(2,1)S(1)}, bf16[1,3,544]{2,1,0:T(4,128)(2,1)}, u32[]{:S(2)}) copy-start(bf16[1,3,544]{2,1,0:T(4,128)(2,1)} %param.10) | copy-start | bytes 9796
  0.0 12.5 %copy-start.4 = (s32[264,1]{0,1:T(1,128)S(1)}, s32[264,1]{0,1:T(1,128)}, u32[]{:S(2)}) copy-start(s32[264,1]{0,1:T(1,128)} %param.17) | copy-start | bytes 3172
  1.6 10.8 %collective-permute-start.2 = (bf16[4,544]{1,0:T(4,128)(2,1)}, bf16[4,544]{1,0:T(4,128)(2,1)S(1)}, u32[]{:S(2)}, u32[]{:S(2)}) collective-permute-start(bf16[4,544]{1,0:T(4,128)(2,1)} %get-tuple-element.8), channel_id=1, source_target_pairs={{0,8},{8,0},{16,24},{24,16},{1,9},{9,1},{17,25},{25,17},{2,10},{10... | collective-permute-start | bytes 13064 | tf_op jit(solution)/shard_map/ppermute | solution.py:406
  4.5 7.9 %collective-permute-start.1 = (bf16[4,544]{1,0:T(4,128)(2,1)}, bf16[4,544]{1,0:T(4,128)(2,1)S(1)}, u32[]{:S(2)}, u32[]{:S(2)}) collective-permute-start(bf16[4,544]{1,0:T(4,128)(2,1)} %get-tuple-element.8), channel_id=1, source_target_pairs={{0,16},{8,24},{16,0},{24,8},{1,17},{9,25},{17,1},{25,9},{2,18},{10... | collective-permute-start | bytes 13064 | tf_op jit(solution)/shard_map/ppermute | solution.py:406
  6.1 6.4 %collective-permute-start = (bf16[4,544]{1,0:T(4,128)(2,1)}, bf16[4,544]{1,0:T(4,128)(2,1)S(1)}, u32[]{:S(2)}, u32[]{:S(2)}) collective-permute-start(bf16[4,544]{1,0:T(4,128)(2,1)} %get-tuple-element.8), channel_id=1, source_target_pairs={{0,24},{8,16},{16,8},{24,0},{1,25},{9,17},{17,9},{25,1},{2,26},{10... | collective-permute-start | bytes 13064 | tf_op jit(solution)/shard_map/ppermute | solution.py:406
  6.1 30.3 %all-to-all-start = ((bf16[32,8,256]{2,1,0:T(8,128)(2,1)}), bf16[32,8,256]{2,1,0:T(8,128)(2,1)S(1)}, u32[]{:S(2)}, u32[]{:S(2)}) async-start(bf16[32,8,256]{2,1,0:T(8,128)(2,1)} %get-tuple-element.7), calls=%async_computation | async-start | bytes 262144 | tf_op jit(solution)/shard_map/all_to_all | solution.py:409
  12.4 24.0 %copy-start.1 = (bf16[2112,152]{0,1:T(8,128)(2,1)S(1)}, bf16[2112,152]{0,1:T(8,128)(2,1)}, u32[]{:S(2)}) copy-start(bf16[2112,152]{0,1:T(8,128)(2,1)} %param.13) | copy-start | bytes 1926148
  12.4 24.0 %copy-start.2 = (s32[1,8]{1,0:T(1,128)S(1)}, s32[1,8]{1,0:T(1,128)}, u32[]{:S(2)}) copy-start(s32[1,8]{1,0:T(1,128)} %refs_0_.1) | copy-start | bytes 100
